TPU v7x, 256 devices: a whole 4x4x8 slice. The times are simulated.
256 devices in a mesh: kpool: 64 (over y, z_lo, x, core), band: 4 (over z_hi).
Axes of the slice: x: 4, y: 4, z: 8 (z_hi: 4, z_lo: 2; z = z_hi * 2 + z_lo), core: 2. Of those that a mesh axis runs over, the one named last changes fastest.
Arguments:
- psi: bfloat16 [64, 2, 4, 48, 2304], P('kpool', None, 'band'), may hold values from -6 to 6
- kpoint_of_pool: int32 [64], replicated, may hold values from 0 to 63, each once
Outputs:
- exchange: float32 [64, 2, 4, 48, 2304], P('kpool', None, 'band')
Inputs may be any that keep to these rules, and one draw needn't show every extreme that they name: `kpoint_of_pool`: each value appears once.
All inputs are finite; a program needn't handle non-finite values.
Results may differ from a plain program's by a relative error of at most 0.0003.
Values may be sent and summed in bfloat16 or wider, within the bound.
No kernel may reach another device: no remote copies, remote signals or barrier semaphores. Data moves between devices by JAX's collectives and lax.ppermute only.
A program may use at most 64 MiB of HBM per device.

v0:
```python
import math

import jax
import jax.numpy as jnp
from jax import lax
from jax.sharding import PartitionSpec as P

GRID = 48
KMESH = 4
ROUNDS = 1


def passed_along(value, axis, by):
    size = lax.axis_size(axis)
    return lax.ppermute(value, axis, [(i, (i + by) % size) for i in range(size)])


def kpoint_coords(labels):
    first = labels % KMESH
    second = labels // KMESH % KMESH
    third = labels // (KMESH * KMESH)
    return jnp.stack([first, second, third], axis=1).astype(jnp.float32) / KMESH


def coulomb(offset):
    index = jnp.arange(GRID, dtype=jnp.int32)
    freq = jnp.where(index < GRID // 2, index, index - GRID).astype(jnp.float32)
    edge = index == GRID // 2
    along_x = (offset[0] + freq) ** 2
    along_y = (offset[1] + freq) ** 2
    along_z = (offset[2] + freq) ** 2
    squared = along_x[:, None, None] + along_y[None, :, None] + along_z[None, None, :]
    cutoff = edge[:, None, None] | edge[None, :, None] | edge[None, None, :]
    safe = jnp.where(cutoff, 1.0, squared)
    amplitude = GRID**1.5 / 16.0
    kernel = jnp.where(cutoff, 0.0, amplitude / safe)
    return kernel.reshape(GRID, GRID * GRID) / (GRID * GRID * GRID)


def stacked_table(cosine, sine):
    upper = jnp.concatenate([cosine, -sine], axis=1)
    lower = jnp.concatenate([sine, cosine], axis=1)
    return jnp.concatenate([upper, lower], axis=0)


def dft_tables():
    index = jnp.arange(GRID, dtype=jnp.int32)
    product = index[:, None] * index[None, :] % GRID
    angles = product.astype(jnp.float32) * (2.0 * math.pi / GRID)
    cosine = jnp.cos(angles)
    sine = jnp.sin(angles)
    return (stacked_table(cosine, -sine), stacked_table(cosine, sine))


def dft_pass(real, imag, table):
    count, size, rest = real.shape
    other = rest // size
    stacked = jnp.concatenate(
        [real.reshape(count, size, size, other), imag.reshape(count, size, size, other)], axis=1
    )
    result = jnp.einsum("ka,mabc->mbck", table, stacked, precision=lax.Precision.HIGHEST)
    out_re = result[..., :size].reshape(count, size, other * size)
    out_im = result[..., size:].reshape(count, size, other * size)
    return (out_re, out_im)


def transform(real, imag, table):
    for _ in range(3):
        real, imag = dft_pass(real, imag, table)
    return (real, imag)


def potential(own_re, own_im, band, kernel, tables):
    band_re = band[0]
    band_im = band[1]
    dens_re = band_re * own_re + band_im * own_im
    dens_im = band_re * own_im - band_im * own_re
    spec_re, spec_im = transform(dens_re, dens_im, tables[0])
    return transform(spec_re * kernel, spec_im * kernel, tables[1])


def own_side(own_re, own_im, kernel, tables):

    def fold(carry, piece, start):

        def step(index, state):
            band = lax.dynamic_index_in_dim(piece, index, 1, keepdims=False).astype(jnp.float32)
            pot_re, pot_im = potential(own_re, own_im, band, kernel, tables)
            new_re = state[0] + band[0] * pot_re - band[1] * pot_im
            new_im = state[1] + band[0] * pot_im + band[1] * pot_re
            return (new_re, new_im)

        return lax.fori_loop(0, piece.shape[1], step, carry)

    return fold


def per_device(psi, kpoint_of_pool):
    own = psi[0]
    band_dev = own.shape[1]
    block = band_dev * lax.axis_size("band")
    pools = lax.axis_size("kpool")
    myself = lax.axis_index("kpool")
    coords = kpoint_coords(kpoint_of_pool)
    here = lax.dynamic_index_in_dim(coords, myself, 0, keepdims=False)
    tables = dft_tables()
    own_re = own[0].astype(jnp.float32)
    own_im = own[1].astype(jnp.float32)
    zeros = jnp.zeros(own_re.shape, jnp.float32)
    total = (zeros, zeros)
    whole_block = lax.all_gather(own, "band", axis=1, tiled=True)
    for direction in (1, -1):
        partner = (myself - direction) % pools
        there = lax.dynamic_index_in_dim(coords, partner, 0, keepdims=False)
        fold = own_side(own_re, own_im, coulomb(here - there), tables)
        arrived = passed_along(whole_block, "kpool", direction * 1)
        total = fold(total, arrived, 0)
    weight = -((2.0 * ROUNDS * block) ** (-0.5))
    result = jnp.stack([total[0], total[1]]) * weight
    return result[None]


def solution(mesh):
    in_specs = (P("kpool", None, "band", None, None), P())
    out_specs = P("kpool", None, "band", None, None)
    return jax.shard_map(
        per_device, mesh=mesh, in_specs=in_specs, out_specs=out_specs, check_vma=False
    )
```

profile of v0, /device:TPU:64, one launch (start us, length us, event | category | flops | bytes accessed | tf_op | source)
XLA Modules:
  0.0 534.0 jit_solution(34386968955332014)
XLA Ops:
  15.2 42.4 %all-gather.3.cloned.1.call-done = bf16[1,2,4,48,2304]{4,3,2,1,0:T(8,128)(2,1)} async-done(((bf16[1,2,1,48,2304]{4,3,2,1,0:T(8,128)(2,1)}), bf16[1,2,4,48,2304]{4,3,2,1,0:T(8,128)(2,1)}) %all-gather.3.cloned.1.call-update) | async-done | bytes 1769488 | tf_op jit(solution)/shard_map/all_gather | solution.py:111
  62.2 5.9 %collective-permute-start.1 = (bf16[2,4,48,2304]{3,2,1,0:T(8,128)(2,1)}, bf16[2,4,48,2304]{3,2,1,0:T(8,128)(2,1)}, u32[]{:S(2)}, u32[]{:S(2)}) collective-permute-start(bf16[2,4,48,2304]{3,2,1,0:T(8,128)(2,1)} %bitcast), channel_id=1, source_target_pairs={{0,252},{4,0},{8,4},{12,8},{16,12},{20,16},{24,20},{28,24},{32,28}... | collective-permute-start | bytes 5308424 | tf_op jit(solution)/shard_map/ppermute | solution.py:15
  68.1 16.0 %collective-permute-done = bf16[2,4,48,2304]{3,2,1,0:T(8,128)(2,1)} collective-permute-done((bf16[2,4,48,2304]{3,2,1,0:T(8,128)(2,1)}, bf16[2,4,48,2304]{3,2,1,0:T(8,128)(2,1)}, u32[]{:S(2)}, u32[]{:S(2)}) %collective-permute-start) | collective-permute-done | bytes 1769504 | tf_op jit(solution)/shard_map/ppermute | solution.py:15
  84.1 210.8 %while.33 = (s32[]{:T(128)}, f32[1,48,2304]{1,2,0:T(8,128)}, f32[1,48,2304]{1,2,0:T(8,128)}, bf16[2,4,48,2304]{3,2,1,0:T(8,128)(2,1)}, f32[1,48,2304]{1,2,0:T(8,...) while((s32[]{:T(128)}, f32[1,48,2304]{1,2,0:T(8,128)}, ...), condition=%wide.region_1.2_spmd.clone, body=%wide.region_0.1_spmd.clone.sunk | while | flops 1533026304 | bytes 49236764 | solution.py:93
  89.9 4.0 fusion.187
  94.5 4.0 fusion.189
  107.7 2.8 reshape.495
  112.9 4.0 fusion.190
  117.5 4.0 fusion.192
  122.1 4.0 fusion.194
  129.1 2.9 copy.129
  132.0 3.6 fusion.196
  142.3 4.0 fusion.187
  146.9 4.0 fusion.189
  160.1 2.8 reshape.495
  165.3 4.0 fusion.190
  169.9 4.0 fusion.192
  174.5 4.0 fusion.194
  181.5 2.9 copy.129
  184.3 4.0 fusion.196
  195.0 4.0 fusion.187
  199.6 4.0 fusion.189
  212.8 2.8 reshape.495
  218.0 4.0 fusion.190
  222.6 4.0 fusion.192
  227.2 4.0 fusion.194
  234.2 2.9 copy.129
  237.1 4.0 fusion.196
  247.7 4.0 fusion.187
  252.3 4.0 fusion.189
  270.7 4.0 fusion.190
  275.3 4.0 fusion.192
  279.9 4.0 fusion.194
  286.9 2.9 copy.129
  289.8 4.0 fusion.196
  294.9 229.0 %while.32 = (s32[]{:T(128)}, f32[1,48,2304]{1,2,0:T(8,128)}, f32[1,48,2304]{1,2,0:T(8,128)}, bf16[2,4,48,2304]{3,2,1,0:T(8,128)(2,1)}, f32[1,48,2304]{1,2,0:T(8,...) while((s32[]{:T(128)}, f32[1,48,2304]{1,2,0:T(8,128)}, ...), condition=%wide.region_3.4_spmd.clone, body=%wide.region_2.3_spmd.clone.sunk | while | flops 1532805120 | bytes 49236748 | solution.py:93
  319.1 4.0 fusion.165
  323.7 4.0 fusion.167
  342.1 4.0 fusion.168
  346.7 4.0 fusion.170
  351.3 4.0 fusion.172
  358.3 2.8 copy.121
  361.1 3.9 fusion.174
  371.7 4.0 fusion.165
  376.3 4.0 fusion.167
  394.7 4.0 fusion.168
  399.3 4.0 fusion.170
  403.9 4.0 fusion.172
  410.9 2.8 copy.121
  413.7 3.9 fusion.174
  424.3 4.0 fusion.165
  428.9 4.0 fusion.167
  447.3 4.0 fusion.168
  451.9 4.0 fusion.170
  456.5 4.0 fusion.172
  463.4 2.8 copy.121
  466.3 3.9 fusion.174
  476.9 4.0 fusion.165
  481.5 4.0 fusion.167
  499.9 4.0 fusion.168
  504.5 4.0 fusion.170
  509.1 4.0 fusion.172
  516.0 2.8 copy.121
  518.9 3.9 fusion.174
  (299 shorter events, 211.8 us)
Async XLA Ops:
  6.5 51.1 %all-gather.3.cloned.1.call-start = ((), (), s32[]{:S(2)}) async-start(), calls=%async_computation | async-start | bytes 2211840 | tf_op jit(solution)/shard_map/all_gather | solution.py:111
  57.6 26.5 %collective-permute-start = (bf16[2,4,48,2304]{3,2,1,0:T(8,128)(2,1)}, bf16[2,4,48,2304]{3,2,1,0:T(8,128)(2,1)}, u32[]{:S(2)}, u32[]{:S(2)}) collective-permute-start(bf16[2,4,48,2304]{3,2,1,0:T(8,128)(2,1)} %bitcast), channel_id=1, source_target_pairs={{0,4},{4,8},{8,12},{12,16},{16,20},{20,24},{24,28},{28,32},{32,36}... | collective-permute-start | bytes 5308424 | tf_op jit(solution)/shard_map/ppermute | solution.py:15
  62.2 232.7 %collective-permute-start.1 = (bf16[2,4,48,2304]{3,2,1,0:T(8,128)(2,1)}, bf16[2,4,48,2304]{3,2,1,0:T(8,128)(2,1)}, u32[]{:S(2)}, u32[]{:S(2)}) collective-permute-start(bf16[2,4,48,2304]{3,2,1,0:T(8,128)(2,1)} %bitcast), channel_id=1, source_target_pairs={{0,252},{4,0},{8,4},{12,8},{16,12},{20,16},{24,20},{28,24},{32,28}... | collective-permute-start | bytes 5308424 | tf_op jit(solution)/shard_map/ppermute | solution.py:15
  86.2 1.9 copy-start.7
  94.5 4.0 copy-start.10
  112.1 0.8 copy-start.5
  129.1 2.9 copy-start
  135.6 1.1 copy-start.1
  138.6 1.9 copy-start.7
  146.8 4.0 copy-start.10
  164.5 0.8 copy-start.5
  181.5 2.9 copy-start
  188.3 1.1 copy-start.1
  191.3 1.9 copy-start.7
  199.6 4.0 copy-start.10
  217.2 0.8 copy-start.5
  234.2 2.9 copy-start
  241.0 1.1 copy-start.1
  244.1 1.9 copy-start.7
  252.3 4.0 copy-start.10
  269.9 0.8 copy-start.5
  286.9 2.9 copy-start
  293.8 1.1 copy-start.1
  315.4 1.9 copy-start.8
  323.7 4.0 copy-start.9
  341.3 0.8 copy-start.6
  358.3 2.8 copy-start.2
  365.0 1.1 copy-start.3
  368.0 1.9 copy-start.8
  376.3 4.0 copy-start.9
  393.9 0.8 copy-start.6
  410.8 2.8 copy-start.2
  417.6 1.1 copy-start.3
  420.6 1.9 copy-start.8
  428.9 4.0 copy-start.9
  446.5 0.8 copy-start.6
  463.4 2.8 copy-start.2
  470.2 1.1 copy-start.3
  473.2 1.9 copy-start.8
  481.5 4.0 copy-start.9
  499.1 0.8 copy-start.6
  516.0 2.8 copy-start.2
  522.8 1.1 copy-start.3
  523.9 1.7 copy-start.4
Sparse Core Ops, SparseCore 0:
  9.2 48.4 all-gather.2
where the time goes:
time: 540 us; the launch traced here: 534 us
  local copies, waits for them, and re-layouts  172 us (32%)
  matrix products  171 us (32%)
  other arithmetic  92.1 us (17%)
  waiting for transfers between devices  59.1 us (11%)
  loops' own time  20.2 us (4%)
  between operations  13.8 us (3%)
  starting transfers between devices  5.97 us (1%)
    dot_general x48, matrix products, dft_pass(): jnp.einsum('ka,mabc->mbck', table, stacked, precision=lax.Precision.HIGHEST)  171 us
    all_gather x1, waiting for transfers between devices, per_device(): whole_block = lax.all_gather(own, 'band', axis=1, tiled=True)  42.4 us
    add x20, local copies, waits for them, and re-layouts, coulomb(): along_x[:, None, None] + along_y[None, :, None] + along_z[None, None, :]  32.4 us
    add x8, other arithmetic, step(): new_im = state[1] + band[0] * pot_im + band[1] * pot_re  31.1 us
    or x18, local copies, waits for them, and re-layouts, coulomb(): cutoff = edge[:, None, None] | edge[None, :, None] | edge[None, None, :]  26.4 us
    slice x40, local copies, waits for them, and re-layouts, dft_pass(): out_re = result[..., :size].reshape(count, size, other * size)  23.3 us
    reshape x8, local copies, waits for them, and re-layouts, dft_pass(): out_re = result[..., :size].reshape(count, size, other * size)  22.8 us
    another operation x8, local copies, waits for them, and re-layouts  22.2 us
  transfers between devices with their start and end apart: 3, of which 2 were waited for; matrix products, arithmetic and copies ran while one was open for 40% of the time, Pallas kernels for 0%

commit v1 on v0

v1 whole, which is shorter than its diff:
```python
import functools
import numpy as np, ml_dtypes
import jax, jax.numpy as jnp
from jax import lax
from jax.experimental import pallas as pl
from jax.sharding import PartitionSpec as P
from jax.experimental.pallas import tpu as pltpu

UN = 24
U1 = 9
U4 = 6
G = 48
YZ = G * G
BF = jnp.bfloat16
F32 = jnp.float32

def split_np(t):
    hi = t.astype(np.float32).astype(ml_dtypes.bfloat16)
    lo = (t - hi.astype(np.float64)).astype(np.float32).astype(ml_dtypes.bfloat16)
    return hi, lo

def tables():
    i = np.arange(G)
    ang = 2 * np.pi * (np.outer(i, i) % G) / G
    c, s = np.cos(ang), np.sin(ang)
    z16 = np.zeros((G, 16))
    fx = np.concatenate([np.concatenate([c, z16, -s, z16], 1), np.concatenate([s, z16, c, z16], 1)], 0)
    hi, lo = split_np(fx)
    tb = np.concatenate([np.concatenate([hi, lo], 1), np.concatenate([hi, np.zeros_like(lo)], 1)], 0)
    def mid(sgn):
        a = np.concatenate([c, sgn * s], 0)
        h, l = split_np(a)
        return np.concatenate([h, h, l], 1)
    ix = np.concatenate([np.concatenate([c, z16, -s, z16], 1), np.concatenate([s, z16, c, z16], 1)], 0)
    h, l = split_np(ix)
    ti = np.concatenate([np.concatenate([h, h], 1), np.concatenate([l, np.zeros_like(l)], 1)], 0)
    return tb, mid(1.0), mid(-1.0), ti

def split(d):
    hi = d.astype(BF)
    return hi, (d - hi.astype(F32)).astype(BF)

def mid_pass(d, table):
    hi, lo = split(d)
    b = jnp.concatenate([hi, lo, hi], axis=0)
    r = jnp.dot(table, b, preferred_element_type=F32)
    out = []
    lane = lax.broadcasted_iota(jnp.int32, (G, 128), 1)
    sg = jnp.where(lane < 64, 1.0, -1.0).astype(F32)
    for k in range(2):
        cpart = r[:G, k * 128:(k + 1) * 128]
        spart = r[G:, k * 128:(k + 1) * 128]
        out.append(cpart + pltpu.roll(spart, 64, 1) * sg)
    return out

def kernel(stages, own_ref, oth_ref, v_ref, tb_ref, tf_ref, tv_ref, ti_ref, acc_in_ref, acc_ref, g1, g2, g3):
    f = pl.program_id(0)

    @pl.when(f == 0)
    def _():
        acc_ref[...] = acc_in_ref[...]

    if 1 in stages:
        @pl.loop(0, 9 // U1)
        def _(jj):
          for h in range(U1):
            sl = pl.ds(pl.multiple_of(jj * (256 * U1) + h * 256, 256), 256)
            pr, pi = own_ref[0, :, sl].astype(F32), own_ref[1, :, sl].astype(F32)
            qr, qi = oth_ref[0, 0, :, sl].astype(F32), oth_ref[0, 1, :, sl].astype(F32)
            dr = qr * pr + qi * pi
            di = qr * pi - qi * pr
            rh, rl = split(dr)
            ih, il = split(di)
            s = jnp.concatenate([rh, ih, rl, il], axis=0)
            r = lax.dot_general(s, tb_ref[...], (((0,), (0,)), ((), ())), preferred_element_type=F32)
            g1[sl, :] = r[:, :128] + r[:, 128:]
    if 2 in stages:
        @pl.loop(0, 24 // UN)
        def _(j):
            for h in range(UN):
                y = j * (2 * UN) + h * 2
                rows = [pl.ds(pl.multiple_of((y + k) * G, G), G) for k in range(2)]
                d = jnp.concatenate([g1[rows[0], :], g1[rows[1], :]], axis=1)
                o = mid_pass(d, tf_ref[...])
                for k in range(2):
                    g2[rows[k], :] = o[k]
    if 3 in stages:
        @pl.loop(0, 24 // UN)
        def _(j):
            for h in range(UN):
                z = j * (2 * UN) + h * 2
                d = jnp.concatenate([g2[pl.ds(z + k, G, stride=G), :] for k in range(2)], axis=1)
                o = mid_pass(d, tf_ref[...])
                d = jnp.concatenate([o[k] * v_ref[0, z + k] for k in range(2)], axis=1)
                o = mid_pass(d, tv_ref[...])
                for k in range(2):
                    g3[pl.ds(pl.multiple_of((z + k) * G, G), G), :] = o[k]
    if 4 in stages:
        @pl.loop(0, 6 // U4)
        def _(jj):
          for hh in range(U4):
            j = jj * U4 + hh
            parts = []
            for h in range(4):
                y = j * 8 + h * 2
                d = jnp.concatenate([g3[pl.ds(y + k, G, stride=G), :] for k in range(2)], axis=1)
                parts += mid_pass(d, tv_ref[...])
            d = jnp.concatenate(parts, axis=0)
            hi, lo = split(d)
            b = jnp.concatenate([hi, lo], axis=1)
            r = lax.dot_general(ti_ref[...], b, (((1,), (1,)), ((), ())), preferred_element_type=F32)
            w = r[:96] + r[96:]
            wr, wi = w[:G], w[G:]
            sl = pl.ds(pl.multiple_of(j * 384, 128), 384)
            qr, qi = oth_ref[0, 0, :, sl].astype(F32), oth_ref[0, 1, :, sl].astype(F32)
            acc_ref[0, :, sl] += qr * wr - qi * wi
            acc_ref[1, :, sl] += qr * wi + qi * wr

def convolve(own, others, v, acc, vmap, stages=(1, 2, 3, 4)):
    nf = others.shape[0]
    tb, tf, tv, ti = tables()
    full = lambda a: pl.BlockSpec(a.shape, lambda f: (0,) * a.ndim)
    return pl.pallas_call(
        functools.partial(kernel, stages),
        grid=(nf,),
        in_specs=[full(own), pl.BlockSpec((1, 2, G, YZ), lambda f: (f, 0, 0, 0)),
                  pl.BlockSpec((1, G, G, 128), lambda f: (vmap(f), 0, 0, 0)),
                  full(tb), full(tf), full(tv), full(ti), full(acc)],
        out_specs=full(acc),
        out_shape=jax.ShapeDtypeStruct(acc.shape, F32),
        scratch_shapes=[pltpu.VMEM((YZ, 128), F32)] * 3,
        compiler_params=pltpu.CompilerParams(vmem_limit_bytes=48 << 20),
    )(own, others, v, jnp.asarray(tb), jnp.asarray(tf), jnp.asarray(tv), jnp.asarray(ti), acc)

def coulomb_zyx(offset):
    index = jnp.arange(G, dtype=jnp.int32)
    freq = jnp.where(index < G // 2, index, index - G).astype(F32)
    lane = jnp.arange(128, dtype=jnp.int32) % 64
    fx = jnp.where(lane < G // 2, lane, lane - G).astype(F32)
    ex = (lane == G // 2) | (lane >= G)
    e = index == G // 2
    ax = (offset[0] + fx) ** 2
    ay = (offset[1] + freq) ** 2
    az = (offset[2] + freq) ** 2
    sq = ax[None, None, :] + ay[None, :, None] + az[:, None, None]
    cut = ex[None, None, :] | e[None, :, None] | e[:, None, None]
    safe = jnp.where(cut, 1.0, sq)
    return jnp.where(cut, 0.0, (G ** 1.5 / 16.0 / G ** 3) / safe)


def kpoint_coords(labels):
    first = labels % 4
    second = labels // 4 % 4
    third = labels // 16
    return jnp.stack([first, second, third], axis=1).astype(F32) / 4


def per_device(psi, kpoint_of_pool):
    own = psi[0, :, 0]
    pools = lax.axis_size("kpool")
    block = lax.axis_size("band")
    myself = lax.axis_index("kpool")
    coords = kpoint_coords(kpoint_of_pool)
    here = lax.dynamic_index_in_dim(coords, myself, 0, keepdims=False)
    weight = -((2.0 * block) ** (-0.5))
    whole = lax.all_gather(own, "band", axis=0)
    acc = jnp.zeros((2, G, YZ), F32)
    for direction in (1, -1):
        partner = (myself - direction) % pools
        there = lax.dynamic_index_in_dim(coords, partner, 0, keepdims=False)
        v = coulomb_zyx(here - there) * weight
        arrived = lax.ppermute(whole, "kpool", [(i, (i + direction) % pools) for i in range(pools)])
        acc = convolve(own, arrived, v[None], acc, lambda f: 0)
    return acc[None, :, None]


def solution(mesh):
    in_specs = (P("kpool", None, "band", None, None), P())
    out_specs = P("kpool", None, "band", None, None)
    return jax.shard_map(per_device, mesh=mesh, in_specs=in_specs, out_specs=out_specs, check_vma=False)
```

time: 540 us -> 127 us (0.24); the launches traced: 534 us -> 127 us
  matrix products: 171 us -> 0 us
  local copies, waits for them, and re-layouts: 172 us -> 1.28 us
  other arithmetic: 92.1 us -> 5.37 us
  Pallas kernels: 0 us -> 36.4 us
  loops' own time: 20.2 us -> 0 us
  waiting for transfers between devices: 59.1 us -> 64.8 us
    dot_general x48 -> x0, matrix products: 171 us -> none  [dft_pass(): jnp.einsum('ka,mabc->mbck', table, stacked, precision=lax.Precision.HIGHEST)]
    add x18 -> x2, other arithmetic: 47.5 us -> 0.14 us  [coulomb_zyx(): sq = ax[None, None, :] + ay[None, :, None] + az[:, None, None]]
    pallas_call x0 -> x2, Pallas kernels: none -> 36.4 us  [convolve(): pl.pallas_call(functools.partial(kernel, stages), grid=(nf,), in_specs=[f...]
    reshape x16 -> x0, local copies, waits for them, and re-layouts: 35 us -> none  [the longest x8 22.8 us: dft_pass(): out_re = result[..., :size].reshape(count, size, other * size)]
    add x20 -> x0, local copies, waits for them, and re-layouts: 32.4 us -> none  [coulomb(): along_x[:, None, None] + along_y[None, :, None] + along_z[None, None, :]]
    or x18 -> x0, local copies, waits for them, and re-layouts: 26.4 us -> none  [coulomb(): cutoff = edge[:, None, None] | edge[None, :, None] | edge[None, None, :]]
    slice x42 -> x2, local copies, waits for them, and re-layouts: 25 us -> 1.19 us  [coulomb_zyx(): ax = (offset[0] + fx) ** 2]
    another operation x8 -> x0, local copies, waits for them, and re-layouts: 22.2 us -> none
  transfers between devices with their start and end apart: 3 -> 3, of which waited for: 2 -> 2; matrix products, arithmetic and copies ran while one was open for 40% -> 5% of each run, Pallas kernels for 0% -> 14%
where the time goes in v1:
time: 127 us
  waiting for transfers between devices  64.8 us (51%)
  Pallas kernels  36.4 us (29%)
  between operations  13.6 us (11%)
  starting transfers between devices  5.97 us (5%)
  other arithmetic  5.37 us (4%)
  local copies, waits for them, and re-layouts  1.28 us (1%)
    all_gather x1, waiting for transfers between devices, per_device(): whole = lax.all_gather(own, 'band', axis=0)  49.5 us
    pallas_call x2, Pallas kernels, convolve(): pl.pallas_call(functools.partial(kernel, stages), grid=(nf,), in_specs=[f...  36.4 us
    ppermute x2, waiting for transfers between devices, per_device(): lax.ppermute(whole, 'kpool', [(i, (i + direction) % pools) for i in range...  14.5 us
    ppermute x2, starting transfers between devices, per_device(): lax.ppermute(whole, 'kpool', [(i, (i + direction) % pools) for i in range...  5.96 us
  transfers between devices with their start and end apart: 3, of which 2 were waited for; matrix products, arithmetic and copies ran while one was open for 5% of the time, Pallas kernels for 14%

profile of v1, /device:TPU:64, one launch (start us, length us, event | category | flops | bytes accessed | tf_op | source)
XLA Modules:
  0.0 127.3 jit_solution(12548482863116725041)
XLA Ops:
  6.5 0.0 all-gather.3.cloned.1.call-start
  6.5 0.7 all-gather.3.cloned.1.call-update
  7.3 0.7 fusion.5
  8.0 0.1 dynamic-slice_subtract_fusion
  8.1 49.5 %all-gather.3.cloned.1.call-done = bf16[4,2,1,48,2304]{4,3,2,1,0:T(8,128)(2,1)} async-done(((bf16[1,2,1,48,2304]{4,3,2,1,0:T(8,128)(2,1)}), bf16[4,2,1,48,2304]{4,3,2,1,0:T(8,128)(2,1)}) %all-gather.3.cloned.1.call-update) | async-done | bytes 1769488 | tf_op jit(solution)/shard_map/all_gather | solution.py:166
  57.6 0.0 collective-permute-start.1
  57.6 5.9 %collective-permute-start = (bf16[4,2,48,2304]{3,2,1,0:T(8,128)(2,1)}, bf16[4,2,48,2304]{3,2,1,0:T(8,128)(2,1)S(1)}, u32[]{:S(2)}, u32[]{:S(2)}) collective-permute-start(bf16[4,2,48,2304]{3,2,1,0:T(8,128)(2,1)} %bitcast.20), channel_id=1, source_target_pairs={{0,252},{4,0},{8,4},{12,8},{16,12},{20,16},{24,20},{28,24},{32,28}... | collective-permute-start | bytes 5308424 | tf_op jit(solution)/shard_map/ppermute | solution.py:172
  63.6 0.6 fusion.11
  64.2 0.7 add_multiply_fusion.1
  64.9 0.6 fusion.12
  65.5 0.6 add_multiply_fusion.4
  66.1 1.2 add_multiply_fusion.2
  67.3 1.2 add_multiply_fusion
  68.6 0.1 broadcast_or_fusion
  68.6 0.1 broadcast_add_fusion.1
  68.7 0.1 broadcast_add_fusion
  68.8 0.0 copy-start
  68.8 0.0 copy-start.1
  68.8 0.0 copy-start.2
  68.8 0.0 copy-start.3
  68.8 0.0 copy-start.4
  68.8 0.6 fusion.3
  69.4 14.5 %collective-permute-done.1.oth_ref = bf16[4,2,48,2304]{3,2,1,0:T(8,128)(2,1)S(1)} collective-permute-done((bf16[4,2,48,2304]{3,2,1,0:T(8,128)(2,1)}, bf16[4,2,48,2304]{3,2,1,0:T(8,128)(2,1)S(1)}, u32[]{:S(2)}, u32[]{:S(2)}) %collective-permute-start.1) | collective-permute-done | bytes 1769504 | tf_op jit(solution)/shard_map/ppermute | solution.py:172
  84.0 0.1 broadcast_in_dim.15.acc_in_ref
  84.0 0.0 copy-done
  84.1 0.0 copy-done.1
  84.1 0.0 copy-done.2
  84.1 0.0 copy-done.3
  84.1 0.0 copy-done.4
  84.1 17.7 %shard_map.100.acc_in_ref = f32[2,48,2304]{2,1,0:T(8,128)S(1)} custom-call(bf16[2,48,2304]{2,1,0:T(8,128)(2,1)S(1)} %bitcast.17, bf16[4,2,48,2304]{3,2,1,0:T(8,128)(2,1)S(1)} %collective-permute-done.1.oth_ref, f32[1,48,48,128]{3,2,1,0:T(8,128)S(1)} %get-tuple-element.5.v_ref, bf16[192,256]{1,0:T(8,128)(2,1)S(1)} %copy-done.2, ...), custom_call_target="tpu_custom_call" | custom-call | tf_op jit(solution)/shard_map/pallas_call | solution.py:123
  101.8 0.0 collective-permute-done.oth_ref
  101.8 18.6 %shard_map.101 = f32[2,48,2304]{2,1,0:T(8,128)} custom-call(bf16[2,48,2304]{2,1,0:T(8,128)(2,1)S(1)} %bitcast.18, bf16[4,2,48,2304]{3,2,1,0:T(8,128)(2,1)S(1)} %collective-permute-done.oth_ref, f32[1,48,48,128]{3,2,1,0:T(8,128)S(1)} %get-tuple-element.6.v_ref, bf16[192,256]{1,0:T(8,128)(2,1)S(1)} %copy-done.2, bf16[96,144]{1,0:T(8,128)(2,1)S(1)} %copy-done.4, ...), custom_call_target="tpu_custom_call" | custom-call | tf_op jit(solution)/shard_map/pallas_call | solution.py:123
  (3 shorter events, 0.0 us)
Async XLA Ops:
  6.5 51.1 %all-gather.3.cloned.1.call-start = ((), (), s32[]{:S(2)}) async-start(), calls=%async_computation | async-start | bytes 2211840 | tf_op jit(solution)/shard_map/all_gather | solution.py:166
  57.6 26.4 %collective-permute-start.1 = (bf16[4,2,48,2304]{3,2,1,0:T(8,128)(2,1)}, bf16[4,2,48,2304]{3,2,1,0:T(8,128)(2,1)S(1)}, u32[]{:S(2)}, u32[]{:S(2)}) collective-permute-start(bf16[4,2,48,2304]{3,2,1,0:T(8,128)(2,1)} %bitcast.19), channel_id=1, source_target_pairs={{0,4},{4,8},{8,12},{12,16},{16,20},{20,24},{24,28},{28,32},{32,36}... | collective-permute-start | bytes 5308424 | tf_op jit(solution)/shard_map/ppermute | solution.py:172
  57.6 44.2 %collective-permute-start = (bf16[4,2,48,2304]{3,2,1,0:T(8,128)(2,1)}, bf16[4,2,48,2304]{3,2,1,0:T(8,128)(2,1)S(1)}, u32[]{:S(2)}, u32[]{:S(2)}) collective-permute-start(bf16[4,2,48,2304]{3,2,1,0:T(8,128)(2,1)} %bitcast.20), channel_id=1, source_target_pairs={{0,252},{4,0},{8,4},{12,8},{16,12},{20,16},{24,20},{28,24},{32,28}... | collective-permute-start | bytes 5308424 | tf_op jit(solution)/shard_map/ppermute | solution.py:172
  68.8 15.3 %copy-start = (bf16[1,2,1,48,2304]{4,3,2,1,0:T(8,128)(2,1)S(1)}, bf16[1,2,1,48,2304]{4,3,2,1,0:T(8,128)(2,1)}, u32[]{:S(2)}) copy-start(bf16[1,2,1,48,2304]{4,3,2,1,0:T(8,128)(2,1)} %param.10) | copy-start | bytes 1327108
  68.8 15.3 %copy-start.1 = (bf16[192,256]{1,0:T(8,128)(2,1)S(1)}, bf16[192,256]{1,0:T(8,128)(2,1)}, u32[]{:S(2)}) copy-start(bf16[192,256]{1,0:T(8,128)(2,1)} %constant.121.clone.ti_ref) | copy-start | bytes 294916
  68.8 15.3 %copy-start.2 = (bf16[192,256]{1,0:T(8,128)(2,1)S(1)}, bf16[192,256]{1,0:T(8,128)(2,1)}, u32[]{:S(2)}) copy-start(bf16[192,256]{1,0:T(8,128)(2,1)} %constant.118.clone.tb_ref) | copy-start | bytes 294916
  68.8 15.3 %copy-start.3 = (bf16[96,144]{1,0:T(8,128)(2,1)S(1)}, bf16[96,144]{1,0:T(8,128)(2,1)}, u32[]{:S(2)}) copy-start(bf16[96,144]{1,0:T(8,128)(2,1)} %constant.120.clone.tv_ref) | copy-start | bytes 82948
  68.8 15.3 %copy-start.4 = (bf16[96,144]{1,0:T(8,128)(2,1)S(1)}, bf16[96,144]{1,0:T(8,128)(2,1)}, u32[]{:S(2)}) copy-start(bf16[96,144]{1,0:T(8,128)(2,1)} %constant.119.clone.tf_ref) | copy-start | bytes 82948
Sparse Core Ops, SparseCore 0:
  9.2 48.4 all-gather.2

commit v2 on v1

v2 whole, which is shorter than its diff:
```python
import functools
import numpy as np, ml_dtypes
import jax, jax.numpy as jnp
from jax import lax
from jax.experimental import pallas as pl
from jax.sharding import PartitionSpec as P
from jax.experimental.pallas import tpu as pltpu

G = 48
YZ = G * G
BF = jnp.bfloat16
F32 = jnp.float32

def split_np(t):
    hi = t.astype(np.float32).astype(ml_dtypes.bfloat16)
    lo = (t - hi.astype(np.float64)).astype(np.float32).astype(ml_dtypes.bfloat16)
    return hi, lo

def tables():
    i = np.arange(G)
    ang = 2 * np.pi * (np.outer(i, i) % G) / G
    c, s = np.cos(ang), np.sin(ang)
    z16 = np.zeros((G, 16))
    fx = np.concatenate([np.concatenate([c, z16, -s, z16], 1), np.concatenate([s, z16, c, z16], 1)], 0)
    hi, lo = split_np(fx)
    tb = np.concatenate([np.concatenate([hi, lo], 1), np.concatenate([hi, np.zeros_like(lo)], 1)], 0)
    def mid(sgn):
        a = np.concatenate([c, sgn * s], 0)
        h, l = split_np(a)
        return np.concatenate([h, h, l], 1)
    ix = np.concatenate([np.concatenate([c, z16, -s, z16], 1), np.concatenate([s, z16, c, z16], 1)], 0)
    h, l = split_np(ix)
    ti = np.concatenate([np.concatenate([h, h], 1), np.concatenate([l, np.zeros_like(l)], 1)], 0)
    return tb, mid(1.0), mid(-1.0), ti

def split(d):
    hi = d.astype(BF)
    return hi, (d - hi.astype(F32)).astype(BF)

def mid_pass(d, table):
    hi, lo = split(d)
    b = jnp.concatenate([hi, lo, hi], axis=0)
    r = jnp.dot(table, b, preferred_element_type=F32)
    out = []
    lane = lax.broadcasted_iota(jnp.int32, (G, 128), 1)
    sg = jnp.where(lane < 64, 1.0, -1.0).astype(F32)
    for k in range(2):
        cpart = r[:G, k * 128:(k + 1) * 128]
        spart = r[G:, k * 128:(k + 1) * 128]
        out.append(cpart + pltpu.roll(spart, 64, 1) * sg)
    return out


def kernel(first, places, own_ref, *rest):
    count = 1 + max(at for at, _ in places)
    arrays, rest = rest[:count], rest[count:]
    fields = [arrays[at] if index is None else arrays[at].at[index] for at, index in places]
    (v_ref, tb_ref, tf_ref, tv_ref, ti_ref), rest = rest[:5], rest[5:]
    acc_in_ref = None if first else rest[0]
    acc_ref, cur, g1, g2, g3, gb = rest if first else rest[1:]
    f = pl.program_id(0)

    @pl.when(f == 0)
    def _():
        acc_ref[...] = jnp.zeros_like(acc_ref) if first else acc_in_ref[...]

    for at, field in enumerate(fields):

        @pl.when(f == at)
        def _():
            cur[...] = field[...]

    for j in range(9):
        sl = slice(j * 256, j * 256 + 256)
        pr, pi = own_ref[0, :, sl].astype(F32), own_ref[1, :, sl].astype(F32)
        qr, qi = cur[0, :, sl].astype(F32), cur[1, :, sl].astype(F32)
        rh, rl = split(qr * pr + qi * pi)
        ih, il = split(qr * pi - qi * pr)
        s = jnp.concatenate([rh, ih, rl, il], axis=0)
        r = lax.dot_general(s, tb_ref[...], (((0,), (0,)), ((), ())), preferred_element_type=F32)
        g1[sl, :] = r[:, :128] + r[:, 128:]
    for y in range(0, G, 2):
        rows = [slice((y + k) * G, (y + k + 1) * G) for k in range(2)]
        o = mid_pass(jnp.concatenate([g1[rows[k], :] for k in range(2)], axis=1), tf_ref[...])
        for k in range(2):
            g2[rows[k], :] = o[k]
    for z in range(0, G, 2):
        d = jnp.concatenate([g2[pl.ds(z + k, G, stride=G), :] for k in range(2)], axis=1)
        o = mid_pass(d, tf_ref[...])
        d = jnp.concatenate([o[k] * v_ref[0, z + k] for k in range(2)], axis=1)
        o = mid_pass(d, tv_ref[...])
        for k in range(2):
            g3[(z + k) * G:(z + k + 1) * G, :] = o[k]
    for y in range(0, G, 2):
        d = jnp.concatenate([g3[pl.ds(y + k, G, stride=G), :] for k in range(2)], axis=1)
        o = mid_pass(d, tv_ref[...])
        for k in range(2):
            rows = slice((y + k) * G, (y + k + 1) * G)
            gb[rows, :128], gb[rows, 128:] = split(o[k])
    for j in range(9):
        sl = slice(j * 256, j * 256 + 256)
        r = lax.dot_general(ti_ref[...], gb[sl, :], (((1,), (1,)), ((), ())), preferred_element_type=F32)
        w = r[:96] + r[96:]
        wr, wi = w[:G], w[G:]
        qr, qi = cur[0, :, sl].astype(F32), cur[1, :, sl].astype(F32)
        acc_ref[0, :, sl] += qr * wr - qi * wi
        acc_ref[1, :, sl] += qr * wi + qi * wr


def convolve(own, fields, sides, v, acc):
    constants = [jnp.asarray(t) for t in tables()]
    first = acc is None
    flat, places = [], []
    for field in fields:
        array, index = field if isinstance(field, tuple) else (field, None)
        known = [k for k, other in enumerate(flat) if other is array]
        places.append((known[0] if known else len(flat), index))
        if not known:
            flat.append(array)
    operands = [own, *flat, v, *constants] + ([] if first else [acc])
    full = lambda t: pl.BlockSpec(t.shape, lambda f: (0,) * t.ndim)
    specs = [full(t) for t in operands]
    step = sides[-1] - sides[0]
    specs[1 + len(flat)] = pl.BlockSpec((1, G, G, 128), lambda f: (sides[0] + f * step, 0, 0, 0))
    shape = jax.ShapeDtypeStruct((2, G, YZ), F32)
    return pl.pallas_call(
        functools.partial(kernel, first, tuple(places)),
        grid=(len(fields),),
        in_specs=specs,
        out_specs=full(shape),
        out_shape=shape,
        scratch_shapes=[pltpu.VMEM((2, G, YZ), BF)] + [pltpu.VMEM((YZ, 128), F32)] * 3 + [pltpu.VMEM((YZ, 256), BF)],
        compiler_params=pltpu.CompilerParams(vmem_limit_bytes=40 << 20),
        cost_estimate=pl.CostEstimate(flops=int(1e8), bytes_accessed=1 << 16, transcendentals=0),
    )(*operands)


def coulomb_zyx(offset):
    index = jnp.arange(G, dtype=jnp.int32)
    freq = jnp.where(index < G // 2, index, index - G).astype(F32)
    lane = jnp.arange(128, dtype=jnp.int32) % 64
    fx = jnp.where(lane < G // 2, lane, lane - G).astype(F32)
    ex = (lane == G // 2) | (lane >= G)
    e = index == G // 2
    ax = (offset[0] + fx) ** 2
    ay = (offset[1] + freq) ** 2
    az = (offset[2] + freq) ** 2
    sq = ax[None, None, :] + ay[None, :, None] + az[:, None, None]
    cut = ex[None, None, :] | e[None, :, None] | e[:, None, None]
    safe = jnp.where(cut, 1.0, sq)
    return jnp.where(cut, 0.0, (G ** 1.5 / 16.0 / G ** 3) / safe)


def kpoint_coords(labels):
    first = labels % 4
    second = labels // 4 % 4
    third = labels // 16
    return jnp.stack([first, second, third], axis=1).astype(F32) / 4


def band_hop(value, by):
    n = lax.axis_size("band")
    return lax.ppermute(value, "band", [(i, (i + by) % n) for i in range(n)])


def swap_chip(value):
    n = lax.axis_size("kpool")
    return lax.ppermute(value, "kpool", [(i, i ^ 1) for i in range(n)])


def swap_next(value):
    n = lax.axis_size("kpool")
    return lax.ppermute(value, "kpool", [(i, (i + 1 if i % 2 else i - 1) % n) for i in range(n)])


def per_device(psi, kpoint_of_pool):
    own = psi[0, :, 0]
    pools = lax.axis_size("kpool")
    block = lax.axis_size("band")
    myself = lax.axis_index("kpool")
    coords = kpoint_coords(kpoint_of_pool)
    at = lambda pool: lax.dynamic_index_in_dim(coords, pool % pools, 0, keepdims=False)
    weight = -((2.0 * block) ** (-0.5))
    odd = myself % 2
    inner = myself + 1 - 2 * odd
    outer = myself - 1 + 2 * odd
    v = jnp.stack([coulomb_zyx(at(myself) - at(s)) * weight for s in (inner, outer)])
    acc = None
    outer, inner = swap_next(own), swap_chip(own)
    up, down = band_hop(own, 1), band_hop(own, -1)
    acc = convolve(own, [inner], [0], v, None)
    up, down, acc = lax.optimization_barrier((up, down, acc))
    across = [band_hop(up[0], 1), band_hop(down[1], -1)]
    both = jnp.stack([up, down])
    inner, outer_both = swap_chip(both), swap_next(both)
    acc = convolve(own, [(inner, 0), (inner, 1)], [0, 0], v, acc)
    acc = convolve(own, [outer], [1], v, acc)
    across, acc = lax.optimization_barrier((across, acc))
    across = jnp.stack(across)
    inner, outer = swap_chip(across), swap_next(across)
    acc = convolve(own, [inner], [0], v, acc)
    acc = convolve(own, [(outer_both, 0), (outer_both, 1)], [1, 1], v, acc)
    acc = convolve(own, [outer], [1], v, acc)
    return acc[None, :, None]


def solution(mesh):
    in_specs = (P("kpool", None, "band", None, None), P())
    out_specs = P("kpool", None, "band", None, None)
    return jax.shard_map(per_device, mesh=mesh, in_specs=in_specs, out_specs=out_specs, check_vma=False)
```

time: 127 us -> 68.4 us (0.54)
  waiting for transfers between devices: 64.8 us -> 10.5 us
  starting transfers between devices: 5.97 us -> 21.8 us
  between operations: 13.6 us -> 0.24 us
  Pallas kernels: 36.4 us -> 27.9 us
    all_gather x1 -> x0, waiting for transfers between devices: 49.5 us -> none  [per_device(): whole = lax.all_gather(own, 'band', axis=0)]
    ppermute x2 -> x10, starting transfers between devices: 5.96 us -> 21.8 us  [the longest x3 14.1 us: swap_next(): lax.ppermute(value, 'kpool', [(i, (i + 1 if i % 2 else i - 1) % n) for i...]
    pallas_call x2 -> x6, Pallas kernels: 36.4 us -> 27.9 us  [convolve(): pl.pallas_call(functools.partial(kernel, first, tuple(places)), grid=(len...]
    ppermute x2 -> x10, waiting for transfers between devices: 14.5 us -> 10.5 us  [the longest x4 7.38 us: band_hop(): return lax.ppermute(value, 'band', [(i, (i + by) % n) for i in range(n)])]
  transfers between devices with their start and end apart: 3 -> 10, of which waited for: 2 -> 3; matrix products, arithmetic and copies ran while one was open for 5% -> 10% of each run, Pallas kernels for 14% -> 35%
where the time goes in v2:
time: 68.4 us; the launch traced here: 68.2 us
  Pallas kernels  27.9 us (41%)
  starting transfers between devices  21.8 us (32%)
  waiting for transfers between devices  10.5 us (15%)
  other arithmetic  5.75 us (8%)
  local copies, waits for them, and re-layouts  2.09 us (3%)
    pallas_call x6, Pallas kernels, convolve(): pl.pallas_call(functools.partial(kernel, first, tuple(places)), grid=(len...  27.9 us
    ppermute x3, starting transfers between devices, swap_next(): lax.ppermute(value, 'kpool', [(i, (i + 1 if i % 2 else i - 1) % n) for i...  14.1 us
    ppermute x4, starting transfers between devices, band_hop(): return lax.ppermute(value, 'band', [(i, (i + by) % n) for i in range(n)])  7.49 us
    ppermute x4, waiting for transfers between devices, band_hop(): return lax.ppermute(value, 'band', [(i, (i + by) % n) for i in range(n)])  7.38 us
    ppermute x3, waiting for transfers between devices, swap_next(): lax.ppermute(value, 'kpool', [(i, (i + 1 if i % 2 else i - 1) % n) for i...  3.14 us
  transfers between devices with their start and end apart: 10, of which 3 were waited for; matrix products, arithmetic and copies ran while one was open for 10% of the time, Pallas kernels for 35%

profile of v2, /device:TPU:64, one launch (start us, length us, event | category | flops | bytes accessed | tf_op | source)
XLA Modules:
  0.0 68.2 jit_solution(13318084801000830679)
XLA Ops:
  0.0 0.0 collective-permute-start.2
  0.0 4.5 %collective-permute-start = (bf16[2,48,2304]{2,1,0:T(8,128)(2,1)}, bf16[2,48,2304]{2,1,0:T(8,128)(2,1)S(1)}, u32[]{:S(2)}, u32[]{:S(2)}) collective-permute-start(bf16[2,48,2304]{2,1,0:T(8,128)(2,1)} %bitcast.25), channel_id=1, source_target_pairs={{0,1},{1,2},{2,3},{3,0},{4,5},{5,6},{6,7},{7,4},{8,9},{9,10},{10,1... | collective-permute-start | bytes 1327112 | tf_op jit(solution)/shard_map/ppermute | solution.py:163
  4.5 0.0 collective-permute-start.1
  4.5 5.5 %collective-permute-start.5 = (bf16[2,48,2304]{2,1,0:T(8,128)(2,1)}, bf16[2,48,2304]{2,1,0:T(8,128)(2,1)S(1)}, u32[]{:S(2)}, u32[]{:S(2)}) collective-permute-start(bf16[2,48,2304]{2,1,0:T(8,128)(2,1)} %bitcast.27), channel_id=1, source_target_pairs={{0,252},{4,8},{8,4},{12,16},{16,12},{20,24},{24,20},{28,32},{32,28... | collective-permute-start | bytes 1327112 | tf_op jit(solution)/shard_map/ppermute | solution.py:173
  10.0 0.7 fusion.5
  10.7 0.1 dynamic-slice_subtract_fusion.1
  10.8 0.6 fusion.11
  11.4 0.6 fusion.12
  12.0 0.7 %add_multiply_fusion.1 = f32[48]{0:T(128)S(1)} fusion(f32[]{:T(128)} %bitcast.8), kind=kLoop, calls=%fused_computation.41 | loop fusion | flops 288 | bytes 196 | tf_op jit(solution)/shard_map/integer_pow | solution.py:146
  12.7 0.6 add_multiply_fusion.4
  13.3 1.3 %add_multiply_fusion.2 = (f32[128]{0:T(128)S(1)}, f32[128]{0:T(128)S(1)}) fusion(f32[]{:T(128)} %bitcast.7, f32[]{:T(128)} %bitcast.4), kind=kLoop, calls=%fused_computation.42 | loop fusion | flops 1792 | bytes 1032 | tf_op jit(solution)/shard_map/integer_pow | solution.py:145
  14.6 0.1 broadcast_add_fusion
  14.7 0.1 broadcast_add_fusion.1
  14.7 1.3 %add_multiply_fusion = (f32[48]{0:T(128)S(1)}, f32[48]{0:T(128)S(1)}) fusion(f32[]{:T(128)} %bitcast.9, f32[]{:T(128)} %bitcast.6), kind=kLoop, calls=%fused_computation.40 | loop fusion | flops 384 | bytes 392 | tf_op jit(solution)/shard_map/integer_pow | solution.py:147
  16.0 0.1 broadcast_or_fusion
  16.1 0.6 fusion.1
  16.7 0.0 copy-start
  16.7 0.0 copy-start.1
  16.7 0.0 copy-start.2
  16.7 0.0 copy-start.3
  16.8 0.0 copy-start.4
  16.8 0.2 pad_maximum_fusion.rest_1_
  16.9 0.0 collective-permute-done.2.rest_0_
  16.9 0.8 %copy-done = bf16[1,2,1,48,2304]{4,3,2,1,0:T(8,128)(2,1)S(1)} copy-done((bf16[1,2,1,48,2304]{4,3,2,1,0:T(8,128)(2,1)S(1)}, bf16[1,2,1,48,2304]{4,3,2,1,0:T(8,128)(2,1)}, u32[]{:S(2)}) %copy-start) | copy-done | bytes 442392
  17.7 0.0 copy-done.1
  17.7 0.0 copy-done.2
  17.8 0.0 copy-done.3
  17.8 0.0 copy-done.4
  17.8 3.3 %shard_map.244.rest_6_ = f32[2,48,2304]{2,1,0:T(8,128)S(1)} custom-call(bf16[2,48,2304]{2,1,0:T(8,128)(2,1)S(1)} %bitcast.28, bf16[2,48,2304]{2,1,0:T(8,128)(2,1)S(1)} %collective-permute-done.2.rest_0_, f32[2,48,48,128]{3,2,1,0:T(8,128)S(1)} %pad_maximum_fusion.rest_1_, bf16[192,256]{1,0:T(8,128)(2,1)S(1)} %copy-done.1, bf16[96,144]{1,0:T(8,128)(2,1)S(1)} %copy-done.3, ...), custom_call_target="tpu_custom_call" | custom-call | flops 100000000 | bytes 65536 | tf_op jit(solution)/shard_map/pallas_call | solution.py:126
  21.1 3.2 %collective-permute-done = bf16[2,48,2304]{2,1,0:T(8,128)(2,1)S(1)} collective-permute-done((bf16[2,48,2304]{2,1,0:T(8,128)(2,1)}, bf16[2,48,2304]{2,1,0:T(8,128)(2,1)S(1)}, u32[]{:S(2)}, u32[]{:S(2)}) %collective-permute-start) | collective-permute-done | bytes 442400 | tf_op jit(solution)/shard_map/ppermute | solution.py:163
  24.3 4.2 %collective-permute-done.1 = bf16[2,48,2304]{2,1,0:T(8,128)(2,1)S(1)} collective-permute-done((bf16[2,48,2304]{2,1,0:T(8,128)(2,1)}, bf16[2,48,2304]{2,1,0:T(8,128)(2,1)S(1)}, u32[]{:S(2)}, u32[]{:S(2)}) %collective-permute-start.1) | collective-permute-done | bytes 442400 | tf_op jit(solution)/shard_map/ppermute | solution.py:163
  28.5 0.1 pad_maximum_fusion.1
  28.6 0.1 collective-permute-start.6
  28.7 0.5 collective-permute-start.3
  29.3 2.5 %collective-permute-start.4 = (bf16[48,2304]{1,0:T(8,128)(2,1)S(1)}, bf16[48,2304]{1,0:T(8,128)(2,1)S(1)}, u32[]{:S(2)}, u32[]{:S(2)}) collective-permute-start(bf16[48,2304]{1,0:T(8,128)(2,1)S(1)} %slice_bitcast_fusion), channel_id=1, source_target_pairs={{0,3},{1,0},{2,1},{3,2},{4,7},{5,4},{6,5},{7,6},{8,11},{9,8},{10,9... | collective-permute-start | bytes 663560 | tf_op jit(solution)/shard_map/ppermute | solution.py:163
  31.7 5.2 %collective-permute-start.8 = (bf16[2,2,48,2304]{3,2,1,0:T(8,128)(2,1)S(1)}, bf16[2,2,48,2304]{3,2,1,0:T(8,128)(2,1)S(1)}, u32[]{:S(2)}, u32[]{:S(2)}) collective-permute-start(bf16[2,2,48,2304]{3,2,1,0:T(8,128)(2,1)S(1)} %pad_maximum_fusion.1), channel_id=1, source_target_pairs={{0,252},{4,8},{8,4},{12,16},{16,12},{20,24},{24,20},{28,32},{32,28... | collective-permute-start | bytes 2654216 | tf_op jit(solution)/shard_map/ppermute | solution.py:173
  36.9 0.0 collective-permute-done.6.rest_0_
  36.9 6.8 %shard_map.245.rest_6_ = f32[2,48,2304]{2,1,0:T(8,128)S(1)} custom-call(bf16[2,48,2304]{2,1,0:T(8,128)(2,1)S(1)} %bitcast.29, bf16[2,2,48,2304]{3,2,1,0:T(8,128)(2,1)S(1)} %collective-permute-done.6.rest_0_, f32[2,48,48,128]{3,2,1,0:T(8,128)S(1)} %pad_maximum_fusion.rest_1_, bf16[192,256]{1,0:T(8,128)(2,1)S(1)} %copy-done.1, bf16[96,144]{1,0:T(8,128)(2,1)S(1)} %copy-done.3, ...), custom_call_target="tpu_custom_call" | custom-call | flops 100000000 | bytes 65536 | tf_op jit(solution)/shard_map/pallas_call | solution.py:126
  43.7 0.0 collective-permute-done.5.rest_0_
  43.7 3.4 %shard_map.246.rest_6_ = f32[2,48,2304]{2,1,0:T(8,128)S(1)} custom-call(bf16[2,48,2304]{2,1,0:T(8,128)(2,1)S(1)} %bitcast.30, bf16[2,48,2304]{2,1,0:T(8,128)(2,1)S(1)} %collective-permute-done.5.rest_0_, f32[2,48,48,128]{3,2,1,0:T(8,128)S(1)} %pad_maximum_fusion.rest_1_, bf16[192,256]{1,0:T(8,128)(2,1)S(1)} %copy-done.1, bf16[96,144]{1,0:T(8,128)(2,1)S(1)} %copy-done.3, ...), custom_call_target="tpu_custom_call" | custom-call | flops 100000000 | bytes 65536 | tf_op jit(solution)/shard_map/pallas_call | solution.py:126
  47.1 0.0 collective-permute-done.3
  47.1 0.0 collective-permute-done.4
  47.2 0.1 collective-permute-start.9
  47.3 3.4 %collective-permute-start.7 = (bf16[2,48,2304]{2,1,0:T(8,128)(2,1)S(1)}, bf16[2,48,2304]{2,1,0:T(8,128)(2,1)S(1)}, u32[]{:S(2)}, u32[]{:S(2)}) collective-permute-start(bf16[2,48,2304]{2,1,0:T(8,128)(2,1)S(1)} %pad_maximum_fusion.2), channel_id=1, source_target_pairs={{0,252},{4,8},{8,4},{12,16},{16,12},{20,24},{24,20},{28,32},{32,28... | collective-permute-start | bytes 1327112 | tf_op jit(solution)/shard_map/ppermute | solution.py:173
  50.7 0.0 collective-permute-done.9.rest_0_
  50.7 3.3 %shard_map.247.rest_6_ = f32[2,48,2304]{2,1,0:T(8,128)S(1)} custom-call(bf16[2,48,2304]{2,1,0:T(8,128)(2,1)S(1)} %bitcast.31, bf16[2,48,2304]{2,1,0:T(8,128)(2,1)S(1)} %collective-permute-done.9.rest_0_, f32[2,48,48,128]{3,2,1,0:T(8,128)S(1)} %pad_maximum_fusion.rest_1_, bf16[192,256]{1,0:T(8,128)(2,1)S(1)} %copy-done.1, bf16[96,144]{1,0:T(8,128)(2,1)S(1)} %copy-done.3, ...), custom_call_target="tpu_custom_call" | custom-call | flops 100000000 | bytes 65536 | tf_op jit(solution)/shard_map/pallas_call | solution.py:126
  54.0 3.1 %collective-permute-done.8.rest_0_ = bf16[2,2,48,2304]{3,2,1,0:T(8,128)(2,1)S(1)} collective-permute-done((bf16[2,2,48,2304]{3,2,1,0:T(8,128)(2,1)S(1)}, bf16[2,2,48,2304]{3,2,1,0:T(8,128)(2,1)S(1)}, u32[]{:S(2)}, u32[]{:S(2)}) %collective-permute-start.8) | collective-permute-done | bytes 884768 | tf_op jit(solution)/shard_map/ppermute | solution.py:173
  57.2 6.8 %shard_map.248.rest_6_ = f32[2,48,2304]{2,1,0:T(8,128)S(1)} custom-call(bf16[2,48,2304]{2,1,0:T(8,128)(2,1)S(1)} %bitcast.32, bf16[2,2,48,2304]{3,2,1,0:T(8,128)(2,1)S(1)} %collective-permute-done.8.rest_0_, f32[2,48,48,128]{3,2,1,0:T(8,128)S(1)} %pad_maximum_fusion.rest_1_, bf16[192,256]{1,0:T(8,128)(2,1)S(1)} %copy-done.1, bf16[96,144]{1,0:T(8,128)(2,1)S(1)} %copy-done.3, ...), custom_call_target="tpu_custom_call" | custom-call | flops 100000000 | bytes 65536 | tf_op jit(solution)/shard_map/pallas_call | solution.py:126
  64.0 0.0 collective-permute-done.7.rest_0_
  64.0 4.2 %shard_map.249 = f32[2,48,2304]{2,1,0:T(8,128)} custom-call(bf16[2,48,2304]{2,1,0:T(8,128)(2,1)S(1)} %bitcast.33, bf16[2,48,2304]{2,1,0:T(8,128)(2,1)S(1)} %collective-permute-done.7.rest_0_, f32[2,48,48,128]{3,2,1,0:T(8,128)S(1)} %pad_maximum_fusion.rest_1_, bf16[192,256]{1,0:T(8,128)(2,1)S(1)} %copy-done.1, bf16[96,144]{1,0:T(8,128)(2,1)S(1)} %copy-done.3, ...), custom_call_target="tpu_custom_call" | custom-call | flops 100000000 | bytes 65536 | tf_op jit(solution)/shard_map/pallas_call | solution.py:126
  (6 shorter events, 0.1 us)
Async XLA Ops:
  0.0 16.9 %collective-permute-start.2 = (bf16[2,48,2304]{2,1,0:T(8,128)(2,1)}, bf16[2,48,2304]{2,1,0:T(8,128)(2,1)S(1)}, u32[]{:S(2)}, u32[]{:S(2)}) collective-permute-start(bf16[2,48,2304]{2,1,0:T(8,128)(2,1)} %bitcast.24), channel_id=1, source_target_pairs={{0,4},{4,0},{8,12},{12,8},{16,20},{20,16},{24,28},{28,24},{32,36},... | collective-permute-start | bytes 1327112 | tf_op jit(solution)/shard_map/ppermute | solution.py:168
  0.0 24.3 %collective-permute-start = (bf16[2,48,2304]{2,1,0:T(8,128)(2,1)}, bf16[2,48,2304]{2,1,0:T(8,128)(2,1)S(1)}, u32[]{:S(2)}, u32[]{:S(2)}) collective-permute-start(bf16[2,48,2304]{2,1,0:T(8,128)(2,1)} %bitcast.25), channel_id=1, source_target_pairs={{0,1},{1,2},{2,3},{3,0},{4,5},{5,6},{6,7},{7,4},{8,9},{9,10},{10,1... | collective-permute-start | bytes 1327112 | tf_op jit(solution)/shard_map/ppermute | solution.py:163
  4.5 24.0 %collective-permute-start.1 = (bf16[2,48,2304]{2,1,0:T(8,128)(2,1)}, bf16[2,48,2304]{2,1,0:T(8,128)(2,1)S(1)}, u32[]{:S(2)}, u32[]{:S(2)}) collective-permute-start(bf16[2,48,2304]{2,1,0:T(8,128)(2,1)} %bitcast.26), channel_id=1, source_target_pairs={{0,3},{1,0},{2,1},{3,2},{4,7},{5,4},{6,5},{7,6},{8,11},{9,8},{10,9... | collective-permute-start | bytes 1327112 | tf_op jit(solution)/shard_map/ppermute | solution.py:163
  4.5 39.2 %collective-permute-start.5 = (bf16[2,48,2304]{2,1,0:T(8,128)(2,1)}, bf16[2,48,2304]{2,1,0:T(8,128)(2,1)S(1)}, u32[]{:S(2)}, u32[]{:S(2)}) collective-permute-start(bf16[2,48,2304]{2,1,0:T(8,128)(2,1)} %bitcast.27), channel_id=1, source_target_pairs={{0,252},{4,8},{8,4},{12,16},{16,12},{20,24},{24,20},{28,32},{32,28... | collective-permute-start | bytes 1327112 | tf_op jit(solution)/shard_map/ppermute | solution.py:173
  16.7 1.0 %copy-start = (bf16[1,2,1,48,2304]{4,3,2,1,0:T(8,128)(2,1)S(1)}, bf16[1,2,1,48,2304]{4,3,2,1,0:T(8,128)(2,1)}, u32[]{:S(2)}) copy-start(bf16[1,2,1,48,2304]{4,3,2,1,0:T(8,128)(2,1)} %param.26) | copy-start | bytes 1327108
  16.7 1.0 %copy-start.1 = (bf16[192,256]{1,0:T(8,128)(2,1)S(1)}, bf16[192,256]{1,0:T(8,128)(2,1)}, u32[]{:S(2)}) copy-start(bf16[192,256]{1,0:T(8,128)(2,1)} %constant.131.clone.rest_2_) | copy-start | bytes 294916
  16.7 1.1 %copy-start.2 = (bf16[192,256]{1,0:T(8,128)(2,1)S(1)}, bf16[192,256]{1,0:T(8,128)(2,1)}, u32[]{:S(2)}) copy-start(bf16[192,256]{1,0:T(8,128)(2,1)} %constant.134.clone.rest_5_) | copy-start | bytes 294916
  16.7 1.0 %copy-start.3 = (bf16[96,144]{1,0:T(8,128)(2,1)S(1)}, bf16[96,144]{1,0:T(8,128)(2,1)}, u32[]{:S(2)}) copy-start(bf16[96,144]{1,0:T(8,128)(2,1)} %constant.132.clone.rest_3_) | copy-start | bytes 82948
  16.8 1.0 %copy-start.4 = (bf16[96,144]{1,0:T(8,128)(2,1)S(1)}, bf16[96,144]{1,0:T(8,128)(2,1)}, u32[]{:S(2)}) copy-start(bf16[96,144]{1,0:T(8,128)(2,1)} %constant.133.clone.rest_4_) | copy-start | bytes 82948
  28.6 8.3 %collective-permute-start.6 = (bf16[2,2,48,2304]{3,2,1,0:T(8,128)(2,1)S(1)}, bf16[2,2,48,2304]{3,2,1,0:T(8,128)(2,1)S(1)}, u32[]{:S(2)}, u32[]{:S(2)}) collective-permute-start(bf16[2,2,48,2304]{3,2,1,0:T(8,128)(2,1)S(1)} %pad_maximum_fusion.1), channel_id=1, source_target_pairs={{0,4},{4,0},{8,12},{12,8},{16,20},{20,16},{24,28},{28,24},{32,36},... | collective-permute-start | bytes 2654216 | tf_op jit(solution)/shard_map/ppermute | solution.py:168
  28.7 18.4 %collective-permute-start.3 = (bf16[48,2304]{1,0:T(8,128)(2,1)S(1)}, bf16[48,2304]{1,0:T(8,128)(2,1)S(1)}, u32[]{:S(2)}, u32[]{:S(2)}) collective-permute-start(bf16[48,2304]{1,0:T(8,128)(2,1)S(1)} %slice_bitcast_fusion.1), channel_id=1, source_target_pairs={{0,1},{1,2},{2,3},{3,0},{4,5},{5,6},{6,7},{7,4},{8,9},{9,10},{10,1... | collective-permute-start | bytes 663560 | tf_op jit(solution)/shard_map/ppermute | solution.py:163
  29.3 17.8 %collective-permute-start.4 = (bf16[48,2304]{1,0:T(8,128)(2,1)S(1)}, bf16[48,2304]{1,0:T(8,128)(2,1)S(1)}, u32[]{:S(2)}, u32[]{:S(2)}) collective-permute-start(bf16[48,2304]{1,0:T(8,128)(2,1)S(1)} %slice_bitcast_fusion), channel_id=1, source_target_pairs={{0,3},{1,0},{2,1},{3,2},{4,7},{5,4},{6,5},{7,6},{8,11},{9,8},{10,9... | collective-permute-start | bytes 663560 | tf_op jit(solution)/shard_map/ppermute | solution.py:163
  31.7 25.4 %collective-permute-start.8 = (bf16[2,2,48,2304]{3,2,1,0:T(8,128)(2,1)S(1)}, bf16[2,2,48,2304]{3,2,1,0:T(8,128)(2,1)S(1)}, u32[]{:S(2)}, u32[]{:S(2)}) collective-permute-start(bf16[2,2,48,2304]{3,2,1,0:T(8,128)(2,1)S(1)} %pad_maximum_fusion.1), channel_id=1, source_target_pairs={{0,252},{4,8},{8,4},{12,16},{16,12},{20,24},{24,20},{28,32},{32,28... | collective-permute-start | bytes 2654216 | tf_op jit(solution)/shard_map/ppermute | solution.py:173
  47.2 3.5 %collective-permute-start.9 = (bf16[2,48,2304]{2,1,0:T(8,128)(2,1)S(1)}, bf16[2,48,2304]{2,1,0:T(8,128)(2,1)S(1)}, u32[]{:S(2)}, u32[]{:S(2)}) collective-permute-start(bf16[2,48,2304]{2,1,0:T(8,128)(2,1)S(1)} %pad_maximum_fusion.2), channel_id=1, source_target_pairs={{0,4},{4,0},{8,12},{12,8},{16,20},{20,16},{24,28},{28,24},{32,36},... | collective-permute-start | bytes 1327112 | tf_op jit(solution)/shard_map/ppermute | solution.py:168
  47.3 16.7 %collective-permute-start.7 = (bf16[2,48,2304]{2,1,0:T(8,128)(2,1)S(1)}, bf16[2,48,2304]{2,1,0:T(8,128)(2,1)S(1)}, u32[]{:S(2)}, u32[]{:S(2)}) collective-permute-start(bf16[2,48,2304]{2,1,0:T(8,128)(2,1)S(1)} %pad_maximum_fusion.2), channel_id=1, source_target_pairs={{0,252},{4,8},{8,4},{12,16},{16,12},{20,24},{24,20},{28,32},{32,28... | collective-permute-start | bytes 1327112 | tf_op jit(solution)/shard_map/ppermute | solution.py:173

commit v3 on v2

--- a/solution.py
+++ b/solution.py
@@ -8,6 +8,7 @@
 
 G = 48
 YZ = G * G
+PITCH = 49
 BF = jnp.bfloat16
 F32 = jnp.float32
 
@@ -83,16 +84,16 @@
         rows = [slice((y + k) * G, (y + k + 1) * G) for k in range(2)]
         o = mid_pass(jnp.concatenate([g1[rows[k], :] for k in range(2)], axis=1), tf_ref[...])
         for k in range(2):
-            g2[rows[k], :] = o[k]
+            g2[(y + k) * PITCH:(y + k) * PITCH + G, :] = o[k]
     for z in range(0, G, 2):
-        d = jnp.concatenate([g2[pl.ds(z + k, G, stride=G), :] for k in range(2)], axis=1)
+        d = jnp.concatenate([g2[pl.ds(z + k, G, stride=PITCH), :] for k in range(2)], axis=1)
         o = mid_pass(d, tf_ref[...])
         d = jnp.concatenate([o[k] * v_ref[0, z + k] for k in range(2)], axis=1)
         o = mid_pass(d, tv_ref[...])
         for k in range(2):
-            g3[(z + k) * G:(z + k + 1) * G, :] = o[k]
+            g3[(z + k) * PITCH:(z + k) * PITCH + G, :] = o[k]
     for y in range(0, G, 2):
-        d = jnp.concatenate([g3[pl.ds(y + k, G, stride=G), :] for k in range(2)], axis=1)
+        d = jnp.concatenate([g3[pl.ds(y + k, G, stride=PITCH), :] for k in range(2)], axis=1)
         o = mid_pass(d, tv_ref[...])
         for k in range(2):
             rows = slice((y + k) * G, (y + k + 1) * G)
@@ -129,7 +130,7 @@
         in_specs=specs,
         out_specs=full(shape),
         out_shape=shape,
-        scratch_shapes=[pltpu.VMEM((2, G, YZ), BF)] + [pltpu.VMEM((YZ, 128), F32)] * 3 + [pltpu.VMEM((YZ, 256), BF)],
+        scratch_shapes=[pltpu.VMEM((2, G, YZ), BF)] + [pltpu.VMEM((YZ, 128), F32)] + [pltpu.VMEM((G * PITCH + 8, 128), F32)] * 2 + [pltpu.VMEM((YZ, 256), BF)],
         compiler_params=pltpu.CompilerParams(vmem_limit_bytes=40 << 20),
         cost_estimate=pl.CostEstimate(flops=int(1e8), bytes_accessed=1 << 16, transcendentals=0),
     )(*operands)
@@ -189,8 +190,10 @@
     outer, inner = swap_next(own), swap_chip(own)
     up, down = band_hop(own, 1), band_hop(own, -1)
     acc = convolve(own, [inner], [0], v, None)
-    up, down, acc = lax.optimization_barrier((up, down, acc))
-    across = [band_hop(up[0], 1), band_hop(down[1], -1)]
+    up, acc = lax.optimization_barrier((up, acc))
+    hop_up = band_hop(up[0], 1)
+    down, acc = lax.optimization_barrier((down, acc))
+    across = [hop_up, band_hop(down[1], -1)]
     both = jnp.stack([up, down])
     inner, outer_both = swap_chip(both), swap_next(both)
     acc = convolve(own, [(inner, 0), (inner, 1)], [0, 0], v, acc)

time: 68.4 us -> 65.3 us (0.955)
  Pallas kernels: 27.9 us -> 26 us
  starting transfers between devices: 21.8 us -> 20.8 us
    ppermute x3, starting transfers between devices: 14.1 us -> 11.9 us  [swap_next(): lax.ppermute(value, 'kpool', [(i, (i + 1 if i % 2 else i - 1) % n) for i...]
    pallas_call x6, Pallas kernels: 27.9 us -> 26 us  [convolve(): pl.pallas_call(functools.partial(kernel, first, tuple(places)), grid=(len...]
    ppermute x4, starting transfers between devices: 7.49 us -> 8.69 us  [band_hop(): return lax.ppermute(value, 'band', [(i, (i + by) % n) for i in range(n)])]
    ppermute x3, waiting for transfers between devices: 3.14 us -> 2.13 us  [swap_next(): lax.ppermute(value, 'kpool', [(i, (i + 1 if i % 2 else i - 1) % n) for i...]
  transfers between devices with their start and end apart: 10 -> 10, of which waited for: 3 -> 4; matrix products, arithmetic and copies ran while one was open for 10% -> 11% of each run, Pallas kernels for 35% -> 34%
where the time goes in v3:
time: 65.3 us; the launch traced here: 65.2 us
  Pallas kernels  26 us (40%)
  starting transfers between devices  20.8 us (32%)
  waiting for transfers between devices  10.3 us (16%)
  other arithmetic  5.75 us (9%)
  local copies, waits for them, and re-layouts  2.09 us (3%)
    pallas_call x6, Pallas kernels, convolve(): pl.pallas_call(functools.partial(kernel, first, tuple(places)), grid=(len...  26 us
    ppermute x3, starting transfers between devices, swap_next(): lax.ppermute(value, 'kpool', [(i, (i + 1 if i % 2 else i - 1) % n) for i...  11.9 us
    ppermute x4, starting transfers between devices, band_hop(): return lax.ppermute(value, 'band', [(i, (i + by) % n) for i in range(n)])  8.69 us
    ppermute x4, waiting for transfers between devices, band_hop(): return lax.ppermute(value, 'band', [(i, (i + by) % n) for i in range(n)])  7.59 us
    ppermute x3, waiting for transfers between devices, swap_next(): lax.ppermute(value, 'kpool', [(i, (i + 1 if i % 2 else i - 1) % n) for i...  2.13 us
    integer_pow x2, other arithmetic, coulomb_zyx(): ay = (offset[1] + freq) ** 2  1.32 us
  transfers between devices with their start and end apart: 10, of which 4 were waited for; matrix products, arithmetic and copies ran while one was open for 11% of the time, Pallas kernels for 34%

profile of v3, /device:TPU:64, one launch (start us, length us, event | category | flops | bytes accessed | tf_op | source)
XLA Modules:
  0.0 65.2 jit_solution(17163861343792813144)
XLA Ops:
  0.0 0.0 collective-permute-start.1
  0.0 4.5 %collective-permute-start = (bf16[2,48,2304]{2,1,0:T(8,128)(2,1)}, bf16[2,48,2304]{2,1,0:T(8,128)(2,1)S(1)}, u32[]{:S(2)}, u32[]{:S(2)}) collective-permute-start(bf16[2,48,2304]{2,1,0:T(8,128)(2,1)} %bitcast.25), channel_id=1, source_target_pairs={{0,1},{1,2},{2,3},{3,0},{4,5},{5,6},{6,7},{7,4},{8,9},{9,10},{10,1... | collective-permute-start | bytes 1327112 | tf_op jit(solution)/shard_map/ppermute | solution.py:164
  4.5 0.0 collective-permute-start.3
  4.5 5.5 %collective-permute-start.5 = (bf16[2,48,2304]{2,1,0:T(8,128)(2,1)}, bf16[2,48,2304]{2,1,0:T(8,128)(2,1)S(1)}, u32[]{:S(2)}, u32[]{:S(2)}) collective-permute-start(bf16[2,48,2304]{2,1,0:T(8,128)(2,1)} %bitcast.27), channel_id=1, source_target_pairs={{0,252},{4,8},{8,4},{12,16},{16,12},{20,24},{24,20},{28,32},{32,28... | collective-permute-start | bytes 1327112 | tf_op jit(solution)/shard_map/ppermute | solution.py:174
  10.0 0.7 %fusion.5 = (s32[64,1]{0,1:T(1,128)S(1)}, s32[64,1]{0,1:T(1,128)S(1)}, s32[64,1]{0,1:T(1,128)S(1)}) fusion(s32[64]{0:T(128)} %param.27), kind=kLoop, calls=%fused_computation.35 | loop fusion | flops 2560 | bytes 1024 | tf_op jit(solution)/shard_map/stack | solution.py:159
  10.7 0.1 dynamic-slice_subtract_fusion.1
  10.8 0.6 fusion.11
  11.4 0.6 fusion.12
  12.0 0.7 %add_multiply_fusion.1 = f32[48]{0:T(128)S(1)} fusion(f32[]{:T(128)} %bitcast.8), kind=kLoop, calls=%fused_computation.41 | loop fusion | flops 288 | bytes 196 | tf_op jit(solution)/shard_map/integer_pow | solution.py:147
  12.7 0.6 add_multiply_fusion.4
  13.3 1.3 %add_multiply_fusion.2 = (f32[128]{0:T(128)S(1)}, f32[128]{0:T(128)S(1)}) fusion(f32[]{:T(128)} %bitcast.7, f32[]{:T(128)} %bitcast.4), kind=kLoop, calls=%fused_computation.42 | loop fusion | flops 1792 | bytes 1032 | tf_op jit(solution)/shard_map/integer_pow | solution.py:146
  14.6 0.1 broadcast_add_fusion
  14.7 0.1 broadcast_add_fusion.1
  14.7 1.3 %add_multiply_fusion = (f32[48]{0:T(128)S(1)}, f32[48]{0:T(128)S(1)}) fusion(f32[]{:T(128)} %bitcast.9, f32[]{:T(128)} %bitcast.6), kind=kLoop, calls=%fused_computation.40 | loop fusion | flops 384 | bytes 392 | tf_op jit(solution)/shard_map/integer_pow | solution.py:148
  16.0 0.1 broadcast_or_fusion
  16.1 0.6 fusion.1
  16.7 0.0 copy-start
  16.7 0.0 copy-start.1
  16.7 0.0 copy-start.2
  16.7 0.0 copy-start.3
  16.8 0.0 copy-start.4
  16.8 0.2 pad_maximum_fusion.rest_1_
  16.9 0.0 collective-permute-done.1.rest_0_
  16.9 0.8 %copy-done = bf16[1,2,1,48,2304]{4,3,2,1,0:T(8,128)(2,1)S(1)} copy-done((bf16[1,2,1,48,2304]{4,3,2,1,0:T(8,128)(2,1)S(1)}, bf16[1,2,1,48,2304]{4,3,2,1,0:T(8,128)(2,1)}, u32[]{:S(2)}) %copy-start) | copy-done | bytes 442392
  17.7 0.0 copy-done.1
  17.7 0.0 copy-done.2
  17.8 0.0 copy-done.3
  17.8 0.0 copy-done.4
  17.8 3.1 %shard_map.244.rest_6_ = f32[2,48,2304]{2,1,0:T(8,128)S(1)} custom-call(bf16[2,48,2304]{2,1,0:T(8,128)(2,1)S(1)} %bitcast.28, bf16[2,48,2304]{2,1,0:T(8,128)(2,1)S(1)} %collective-permute-done.1.rest_0_, f32[2,48,48,128]{3,2,1,0:T(8,128)S(1)} %pad_maximum_fusion.rest_1_, bf16[192,256]{1,0:T(8,128)(2,1)S(1)} %copy-done.1, bf16[96,144]{1,0:T(8,128)(2,1)S(1)} %copy-done.3, ...), custom_call_target="tpu_custom_call" | custom-call | flops 100000000 | bytes 65536 | tf_op jit(solution)/shard_map/pallas_call | solution.py:127
  20.9 3.4 %collective-permute-done = bf16[2,48,2304]{2,1,0:T(8,128)(2,1)S(1)} collective-permute-done((bf16[2,48,2304]{2,1,0:T(8,128)(2,1)}, bf16[2,48,2304]{2,1,0:T(8,128)(2,1)S(1)}, u32[]{:S(2)}, u32[]{:S(2)}) %collective-permute-start) | collective-permute-done | bytes 442400 | tf_op jit(solution)/shard_map/ppermute | solution.py:164
  24.3 4.2 %collective-permute-done.3 = bf16[2,48,2304]{2,1,0:T(8,128)(2,1)S(1)} collective-permute-done((bf16[2,48,2304]{2,1,0:T(8,128)(2,1)}, bf16[2,48,2304]{2,1,0:T(8,128)(2,1)S(1)}, u32[]{:S(2)}, u32[]{:S(2)}) %collective-permute-start.3) | collective-permute-done | bytes 442400 | tf_op jit(solution)/shard_map/ppermute | solution.py:164
  28.5 0.1 pad_maximum_fusion.1
  28.6 0.1 collective-permute-start.6
  28.7 0.1 collective-permute-start.4
  28.8 4.1 %collective-permute-start.2 = (bf16[48,2304]{1,0:T(8,128)(2,1)S(1)}, bf16[48,2304]{1,0:T(8,128)(2,1)S(1)}, u32[]{:S(2)}, u32[]{:S(2)}) collective-permute-start(bf16[48,2304]{1,0:T(8,128)(2,1)S(1)} %slice_bitcast_fusion.1), channel_id=1, source_target_pairs={{0,1},{1,2},{2,3},{3,0},{4,5},{5,6},{6,7},{7,4},{8,9},{9,10},{10,1... | collective-permute-start | bytes 663560 | tf_op jit(solution)/shard_map/ppermute | solution.py:164
  32.9 5.2 %collective-permute-start.8 = (bf16[2,2,48,2304]{3,2,1,0:T(8,128)(2,1)S(1)}, bf16[2,2,48,2304]{3,2,1,0:T(8,128)(2,1)S(1)}, u32[]{:S(2)}, u32[]{:S(2)}) collective-permute-start(bf16[2,2,48,2304]{3,2,1,0:T(8,128)(2,1)S(1)} %pad_maximum_fusion.1), channel_id=1, source_target_pairs={{0,252},{4,8},{8,4},{12,16},{16,12},{20,24},{24,20},{28,32},{32,28... | collective-permute-start | bytes 2654216 | tf_op jit(solution)/shard_map/ppermute | solution.py:174
  38.1 0.0 collective-permute-done.6.rest_0_
  38.1 6.3 %shard_map.245.rest_6_ = f32[2,48,2304]{2,1,0:T(8,128)S(1)} custom-call(bf16[2,48,2304]{2,1,0:T(8,128)(2,1)S(1)} %bitcast.29, bf16[2,2,48,2304]{3,2,1,0:T(8,128)(2,1)S(1)} %collective-permute-done.6.rest_0_, f32[2,48,48,128]{3,2,1,0:T(8,128)S(1)} %pad_maximum_fusion.rest_1_, bf16[192,256]{1,0:T(8,128)(2,1)S(1)} %copy-done.1, bf16[96,144]{1,0:T(8,128)(2,1)S(1)} %copy-done.3, ...), custom_call_target="tpu_custom_call" | custom-call | flops 100000000 | bytes 65536 | tf_op jit(solution)/shard_map/pallas_call | solution.py:127
  44.5 0.0 collective-permute-done.5.rest_0_
  44.5 3.1 %shard_map.246.rest_6_ = f32[2,48,2304]{2,1,0:T(8,128)S(1)} custom-call(bf16[2,48,2304]{2,1,0:T(8,128)(2,1)S(1)} %bitcast.30, bf16[2,48,2304]{2,1,0:T(8,128)(2,1)S(1)} %collective-permute-done.5.rest_0_, f32[2,48,48,128]{3,2,1,0:T(8,128)S(1)} %pad_maximum_fusion.rest_1_, bf16[192,256]{1,0:T(8,128)(2,1)S(1)} %copy-done.1, bf16[96,144]{1,0:T(8,128)(2,1)S(1)} %copy-done.3, ...), custom_call_target="tpu_custom_call" | custom-call | flops 100000000 | bytes 65536 | tf_op jit(solution)/shard_map/pallas_call | solution.py:127
  47.6 0.0 collective-permute-done.4
  47.6 0.0 collective-permute-done.2
  47.7 0.1 collective-permute-start.9
  47.8 1.2 %collective-permute-start.7 = (bf16[2,48,2304]{2,1,0:T(8,128)(2,1)S(1)}, bf16[2,48,2304]{2,1,0:T(8,128)(2,1)S(1)}, u32[]{:S(2)}, u32[]{:S(2)}) collective-permute-start(bf16[2,48,2304]{2,1,0:T(8,128)(2,1)S(1)} %pad_maximum_fusion.2), channel_id=1, source_target_pairs={{0,252},{4,8},{8,4},{12,16},{16,12},{20,24},{24,20},{28,32},{32,28... | collective-permute-start | bytes 1327112 | tf_op jit(solution)/shard_map/ppermute | solution.py:174
  49.0 0.5 collective-permute-done.9.rest_0_
  49.6 3.1 %shard_map.247.rest_6_ = f32[2,48,2304]{2,1,0:T(8,128)S(1)} custom-call(bf16[2,48,2304]{2,1,0:T(8,128)(2,1)S(1)} %bitcast.31, bf16[2,48,2304]{2,1,0:T(8,128)(2,1)S(1)} %collective-permute-done.9.rest_0_, f32[2,48,48,128]{3,2,1,0:T(8,128)S(1)} %pad_maximum_fusion.rest_1_, bf16[192,256]{1,0:T(8,128)(2,1)S(1)} %copy-done.1, bf16[96,144]{1,0:T(8,128)(2,1)S(1)} %copy-done.3, ...), custom_call_target="tpu_custom_call" | custom-call | flops 100000000 | bytes 65536 | tf_op jit(solution)/shard_map/pallas_call | solution.py:127
  52.7 2.1 %collective-permute-done.8.rest_0_ = bf16[2,2,48,2304]{3,2,1,0:T(8,128)(2,1)S(1)} collective-permute-done((bf16[2,2,48,2304]{3,2,1,0:T(8,128)(2,1)S(1)}, bf16[2,2,48,2304]{3,2,1,0:T(8,128)(2,1)S(1)}, u32[]{:S(2)}, u32[]{:S(2)}) %collective-permute-start.8) | collective-permute-done | bytes 884768 | tf_op jit(solution)/shard_map/ppermute | solution.py:174
  54.8 6.3 %shard_map.248.rest_6_ = f32[2,48,2304]{2,1,0:T(8,128)S(1)} custom-call(bf16[2,48,2304]{2,1,0:T(8,128)(2,1)S(1)} %bitcast.32, bf16[2,2,48,2304]{3,2,1,0:T(8,128)(2,1)S(1)} %collective-permute-done.8.rest_0_, f32[2,48,48,128]{3,2,1,0:T(8,128)S(1)} %pad_maximum_fusion.rest_1_, bf16[192,256]{1,0:T(8,128)(2,1)S(1)} %copy-done.1, bf16[96,144]{1,0:T(8,128)(2,1)S(1)} %copy-done.3, ...), custom_call_target="tpu_custom_call" | custom-call | flops 100000000 | bytes 65536 | tf_op jit(solution)/shard_map/pallas_call | solution.py:127
  61.1 0.0 collective-permute-done.7.rest_0_
  61.1 4.0 %shard_map.249 = f32[2,48,2304]{2,1,0:T(8,128)} custom-call(bf16[2,48,2304]{2,1,0:T(8,128)(2,1)S(1)} %bitcast.33, bf16[2,48,2304]{2,1,0:T(8,128)(2,1)S(1)} %collective-permute-done.7.rest_0_, f32[2,48,48,128]{3,2,1,0:T(8,128)S(1)} %pad_maximum_fusion.rest_1_, bf16[192,256]{1,0:T(8,128)(2,1)S(1)} %copy-done.1, bf16[96,144]{1,0:T(8,128)(2,1)S(1)} %copy-done.3, ...), custom_call_target="tpu_custom_call" | custom-call | flops 100000000 | bytes 65536 | tf_op jit(solution)/shard_map/pallas_call | solution.py:127
  (6 shorter events, 0.1 us)
Async XLA Ops:
  0.0 16.9 %collective-permute-start.1 = (bf16[2,48,2304]{2,1,0:T(8,128)(2,1)}, bf16[2,48,2304]{2,1,0:T(8,128)(2,1)S(1)}, u32[]{:S(2)}, u32[]{:S(2)}) collective-permute-start(bf16[2,48,2304]{2,1,0:T(8,128)(2,1)} %bitcast.24), channel_id=1, source_target_pairs={{0,4},{4,0},{8,12},{12,8},{16,20},{20,16},{24,28},{28,24},{32,36},... | collective-permute-start | bytes 1327112 | tf_op jit(solution)/shard_map/ppermute | solution.py:169
  0.0 24.3 %collective-permute-start = (bf16[2,48,2304]{2,1,0:T(8,128)(2,1)}, bf16[2,48,2304]{2,1,0:T(8,128)(2,1)S(1)}, u32[]{:S(2)}, u32[]{:S(2)}) collective-permute-start(bf16[2,48,2304]{2,1,0:T(8,128)(2,1)} %bitcast.25), channel_id=1, source_target_pairs={{0,1},{1,2},{2,3},{3,0},{4,5},{5,6},{6,7},{7,4},{8,9},{9,10},{10,1... | collective-permute-start | bytes 1327112 | tf_op jit(solution)/shard_map/ppermute | solution.py:164
  4.5 24.0 %collective-permute-start.3 = (bf16[2,48,2304]{2,1,0:T(8,128)(2,1)}, bf16[2,48,2304]{2,1,0:T(8,128)(2,1)S(1)}, u32[]{:S(2)}, u32[]{:S(2)}) collective-permute-start(bf16[2,48,2304]{2,1,0:T(8,128)(2,1)} %bitcast.26), channel_id=1, source_target_pairs={{0,3},{1,0},{2,1},{3,2},{4,7},{5,4},{6,5},{7,6},{8,11},{9,8},{10,9... | collective-permute-start | bytes 1327112 | tf_op jit(solution)/shard_map/ppermute | solution.py:164
  4.5 40.0 %collective-permute-start.5 = (bf16[2,48,2304]{2,1,0:T(8,128)(2,1)}, bf16[2,48,2304]{2,1,0:T(8,128)(2,1)S(1)}, u32[]{:S(2)}, u32[]{:S(2)}) collective-permute-start(bf16[2,48,2304]{2,1,0:T(8,128)(2,1)} %bitcast.27), channel_id=1, source_target_pairs={{0,252},{4,8},{8,4},{12,16},{16,12},{20,24},{24,20},{28,32},{32,28... | collective-permute-start | bytes 1327112 | tf_op jit(solution)/shard_map/ppermute | solution.py:174
  16.7 1.0 %copy-start = (bf16[1,2,1,48,2304]{4,3,2,1,0:T(8,128)(2,1)S(1)}, bf16[1,2,1,48,2304]{4,3,2,1,0:T(8,128)(2,1)}, u32[]{:S(2)}) copy-start(bf16[1,2,1,48,2304]{4,3,2,1,0:T(8,128)(2,1)} %param.26) | copy-start | bytes 1327108
  16.7 1.0 %copy-start.1 = (bf16[192,256]{1,0:T(8,128)(2,1)S(1)}, bf16[192,256]{1,0:T(8,128)(2,1)}, u32[]{:S(2)}) copy-start(bf16[192,256]{1,0:T(8,128)(2,1)} %constant.131.clone.rest_2_) | copy-start | bytes 294916
  16.7 1.1 %copy-start.2 = (bf16[192,256]{1,0:T(8,128)(2,1)S(1)}, bf16[192,256]{1,0:T(8,128)(2,1)}, u32[]{:S(2)}) copy-start(bf16[192,256]{1,0:T(8,128)(2,1)} %constant.134.clone.rest_5_) | copy-start | bytes 294916
  16.7 1.0 %copy-start.3 = (bf16[96,144]{1,0:T(8,128)(2,1)S(1)}, bf16[96,144]{1,0:T(8,128)(2,1)}, u32[]{:S(2)}) copy-start(bf16[96,144]{1,0:T(8,128)(2,1)} %constant.132.clone.rest_3_) | copy-start | bytes 82948
  16.8 1.0 %copy-start.4 = (bf16[96,144]{1,0:T(8,128)(2,1)S(1)}, bf16[96,144]{1,0:T(8,128)(2,1)}, u32[]{:S(2)}) copy-start(bf16[96,144]{1,0:T(8,128)(2,1)} %constant.133.clone.rest_4_) | copy-start | bytes 82948
  28.6 9.5 %collective-permute-start.6 = (bf16[2,2,48,2304]{3,2,1,0:T(8,128)(2,1)S(1)}, bf16[2,2,48,2304]{3,2,1,0:T(8,128)(2,1)S(1)}, u32[]{:S(2)}, u32[]{:S(2)}) collective-permute-start(bf16[2,2,48,2304]{3,2,1,0:T(8,128)(2,1)S(1)} %pad_maximum_fusion.1), channel_id=1, source_target_pairs={{0,4},{4,0},{8,12},{12,8},{16,20},{20,16},{24,28},{28,24},{32,36},... | collective-permute-start | bytes 2654216 | tf_op jit(solution)/shard_map/ppermute | solution.py:169
  28.7 18.9 %collective-permute-start.4 = (bf16[48,2304]{1,0:T(8,128)(2,1)S(1)}, bf16[48,2304]{1,0:T(8,128)(2,1)S(1)}, u32[]{:S(2)}, u32[]{:S(2)}) collective-permute-start(bf16[48,2304]{1,0:T(8,128)(2,1)S(1)} %slice_bitcast_fusion), channel_id=1, source_target_pairs={{0,3},{1,0},{2,1},{3,2},{4,7},{5,4},{6,5},{7,6},{8,11},{9,8},{10,9... | collective-permute-start | bytes 663560 | tf_op jit(solution)/shard_map/ppermute | solution.py:164
  28.8 18.8 %collective-permute-start.2 = (bf16[48,2304]{1,0:T(8,128)(2,1)S(1)}, bf16[48,2304]{1,0:T(8,128)(2,1)S(1)}, u32[]{:S(2)}, u32[]{:S(2)}) collective-permute-start(bf16[48,2304]{1,0:T(8,128)(2,1)S(1)} %slice_bitcast_fusion.1), channel_id=1, source_target_pairs={{0,1},{1,2},{2,3},{3,0},{4,5},{5,6},{6,7},{7,4},{8,9},{9,10},{10,1... | collective-permute-start | bytes 663560 | tf_op jit(solution)/shard_map/ppermute | solution.py:164
  32.9 21.9 %collective-permute-start.8 = (bf16[2,2,48,2304]{3,2,1,0:T(8,128)(2,1)S(1)}, bf16[2,2,48,2304]{3,2,1,0:T(8,128)(2,1)S(1)}, u32[]{:S(2)}, u32[]{:S(2)}) collective-permute-start(bf16[2,2,48,2304]{3,2,1,0:T(8,128)(2,1)S(1)} %pad_maximum_fusion.1), channel_id=1, source_target_pairs={{0,252},{4,8},{8,4},{12,16},{16,12},{20,24},{24,20},{28,32},{32,28... | collective-permute-start | bytes 2654216 | tf_op jit(solution)/shard_map/ppermute | solution.py:174
  47.7 1.9 %collective-permute-start.9 = (bf16[2,48,2304]{2,1,0:T(8,128)(2,1)S(1)}, bf16[2,48,2304]{2,1,0:T(8,128)(2,1)S(1)}, u32[]{:S(2)}, u32[]{:S(2)}) collective-permute-start(bf16[2,48,2304]{2,1,0:T(8,128)(2,1)S(1)} %pad_maximum_fusion.2), channel_id=1, source_target_pairs={{0,4},{4,0},{8,12},{12,8},{16,20},{20,16},{24,28},{28,24},{32,36},... | collective-permute-start | bytes 1327112 | tf_op jit(solution)/shard_map/ppermute | solution.py:169
  47.8 13.4 %collective-permute-start.7 = (bf16[2,48,2304]{2,1,0:T(8,128)(2,1)S(1)}, bf16[2,48,2304]{2,1,0:T(8,128)(2,1)S(1)}, u32[]{:S(2)}, u32[]{:S(2)}) collective-permute-start(bf16[2,48,2304]{2,1,0:T(8,128)(2,1)S(1)} %pad_maximum_fusion.2), channel_id=1, source_target_pairs={{0,252},{4,8},{8,4},{12,16},{16,12},{20,24},{24,20},{28,32},{32,28... | collective-permute-start | bytes 1327112 | tf_op jit(solution)/shard_map/ppermute | solution.py:174

commit v4 on v3

--- a/solution.py
+++ b/solution.py
@@ -191,12 +191,12 @@
     up, down = band_hop(own, 1), band_hop(own, -1)
     acc = convolve(own, [inner], [0], v, None)
     up, acc = lax.optimization_barrier((up, acc))
-    hop_up = band_hop(up[0], 1)
+    hop_up, inner_up = band_hop(up[0], 1), swap_chip(up)
     down, acc = lax.optimization_barrier((down, acc))
     across = [hop_up, band_hop(down[1], -1)]
     both = jnp.stack([up, down])
-    inner, outer_both = swap_chip(both), swap_next(both)
-    acc = convolve(own, [(inner, 0), (inner, 1)], [0, 0], v, acc)
+    inner_down, outer_both = swap_chip(down), swap_next(both)
+    acc = convolve(own, [inner_up, inner_down], [0, 0], v, acc)
     acc = convolve(own, [outer], [1], v, acc)
     across, acc = lax.optimization_barrier((across, acc))
     across = jnp.stack(across)

time: 65.3 us -> 65.3 us (level)
  transfers between devices with their start and end apart: 10 -> 11, of which waited for: 4 -> 4; matrix products, arithmetic and copies ran while one was open for 11% -> 11% of each run, Pallas kernels for 34% -> 34%
where the time goes in v4:
time: 65.3 us; the launch traced here: 65.1 us
  Pallas kernels  26 us (40%)
  starting transfers between devices  21.4 us (33%)
  waiting for transfers between devices  9.65 us (15%)
  other arithmetic  5.7 us (9%)
  local copies, waits for them, and re-layouts  2.08 us (3%)
    pallas_call x6, Pallas kernels, convolve(): pl.pallas_call(functools.partial(kernel, first, tuple(places)), grid=(len...  26 us
    ppermute x3, starting transfers between devices, swap_next(): lax.ppermute(value, 'kpool', [(i, (i + 1 if i % 2 else i - 1) % n) for i...  12 us
    ppermute x4, starting transfers between devices, band_hop(): return lax.ppermute(value, 'band', [(i, (i + by) % n) for i in range(n)])  8.69 us
    ppermute x4, waiting for transfers between devices, band_hop(): return lax.ppermute(value, 'band', [(i, (i + by) % n) for i in range(n)])  7.66 us
    ppermute x3, waiting for transfers between devices, swap_next(): lax.ppermute(value, 'kpool', [(i, (i + 1 if i % 2 else i - 1) % n) for i...  1.76 us
    integer_pow x1, other arithmetic, coulomb_zyx(): az = (offset[2] + freq) ** 2  1.32 us
  transfers between devices with their start and end apart: 11, of which 4 were waited for; matrix products, arithmetic and copies ran while one was open for 11% of the time, Pallas kernels for 34%

profile of v4, /device:TPU:64, one launch (start us, length us, event | category | flops | bytes accessed | tf_op | source)
XLA Modules:
  0.0 65.1 jit_solution(10171488441928402543)
XLA Ops:
  0.0 0.0 collective-permute-start.1
  0.0 4.5 %collective-permute-start = (bf16[2,48,2304]{2,1,0:T(8,128)(2,1)}, bf16[2,48,2304]{2,1,0:T(8,128)(2,1)S(1)}, u32[]{:S(2)}, u32[]{:S(2)}) collective-permute-start(bf16[2,48,2304]{2,1,0:T(8,128)(2,1)} %bitcast.25), channel_id=1, source_target_pairs={{0,1},{1,2},{2,3},{3,0},{4,5},{5,6},{6,7},{7,4},{8,9},{9,10},{10,1... | collective-permute-start | bytes 1327112 | tf_op jit(solution)/shard_map/ppermute | solution.py:164
  4.5 0.0 collective-permute-start.3
  4.5 5.5 %collective-permute-start.5 = (bf16[2,48,2304]{2,1,0:T(8,128)(2,1)}, bf16[2,48,2304]{2,1,0:T(8,128)(2,1)S(1)}, u32[]{:S(2)}, u32[]{:S(2)}) collective-permute-start(bf16[2,48,2304]{2,1,0:T(8,128)(2,1)} %bitcast.27), channel_id=1, source_target_pairs={{0,252},{4,8},{8,4},{12,16},{16,12},{20,24},{24,20},{28,32},{32,28... | collective-permute-start | bytes 1327112 | tf_op jit(solution)/shard_map/ppermute | solution.py:174
  10.0 0.7 %fusion.5 = (s32[64,1]{0,1:T(1,128)S(1)}, s32[64,1]{0,1:T(1,128)S(1)}, s32[64,1]{0,1:T(1,128)S(1)}) fusion(s32[64]{0:T(128)} %param.27), kind=kLoop, calls=%fused_computation.35 | loop fusion | flops 2560 | bytes 1024 | tf_op jit(solution)/shard_map/stack | solution.py:159
  10.7 0.1 dynamic-slice_subtract_fusion.1
  10.8 0.6 fusion.11
  11.4 0.6 fusion.12
  12.0 0.6 add_multiply_fusion.1
  12.6 0.6 add_multiply_fusion.4
  13.2 1.3 %add_multiply_fusion.2 = (f32[128]{0:T(128)S(1)}, f32[128]{0:T(128)S(1)}) fusion(f32[]{:T(128)} %bitcast.7, f32[]{:T(128)} %bitcast.4), kind=kLoop, calls=%fused_computation.42 | loop fusion | flops 1792 | bytes 1032 | tf_op jit(solution)/shard_map/integer_pow | solution.py:146
  14.5 0.1 broadcast_add_fusion
  14.5 0.1 broadcast_add_fusion.1
  14.6 1.3 %add_multiply_fusion = (f32[48]{0:T(128)S(1)}, f32[48]{0:T(128)S(1)}) fusion(f32[]{:T(128)} %bitcast.9, f32[]{:T(128)} %bitcast.6), kind=kLoop, calls=%fused_computation.40 | loop fusion | flops 384 | bytes 392 | tf_op jit(solution)/shard_map/integer_pow | solution.py:148
  15.9 0.1 broadcast_or_fusion
  16.0 0.6 fusion.1
  16.6 0.0 copy-start
  16.7 0.0 copy-start.1
  16.7 0.0 copy-start.2
  16.7 0.0 copy-start.3
  16.7 0.0 copy-start.4
  16.7 0.2 pad_maximum_fusion.rest_1_.rest_2_
  16.9 0.0 collective-permute-done.1.rest_0_
  16.9 0.8 %copy-done = bf16[1,2,1,48,2304]{4,3,2,1,0:T(8,128)(2,1)S(1)} copy-done((bf16[1,2,1,48,2304]{4,3,2,1,0:T(8,128)(2,1)S(1)}, bf16[1,2,1,48,2304]{4,3,2,1,0:T(8,128)(2,1)}, u32[]{:S(2)}) %copy-start) | copy-done | bytes 442392
  17.7 0.0 copy-done.1
  17.7 0.0 copy-done.2
  17.7 0.0 copy-done.3
  17.7 0.0 copy-done.4
  17.7 3.1 %shard_map.244.rest_7_ = f32[2,48,2304]{2,1,0:T(8,128)S(1)} custom-call(bf16[2,48,2304]{2,1,0:T(8,128)(2,1)S(1)} %bitcast.28, bf16[2,48,2304]{2,1,0:T(8,128)(2,1)S(1)} %collective-permute-done.1.rest_0_, f32[2,48,48,128]{3,2,1,0:T(8,128)S(1)} %pad_maximum_fusion.rest_1_.rest_2_, bf16[192,256]{1,0:T(8,128)(2,1)S(1)} %copy-done.1, ...), custom_call_target="tpu_custom_call" | custom-call | flops 100000000 | bytes 65536 | tf_op jit(solution)/shard_map/pallas_call | solution.py:127
  20.8 3.4 %collective-permute-done = bf16[2,48,2304]{2,1,0:T(8,128)(2,1)S(1)} collective-permute-done((bf16[2,48,2304]{2,1,0:T(8,128)(2,1)}, bf16[2,48,2304]{2,1,0:T(8,128)(2,1)S(1)}, u32[]{:S(2)}, u32[]{:S(2)}) %collective-permute-start) | collective-permute-done | bytes 442400 | tf_op jit(solution)/shard_map/ppermute | solution.py:164
  24.3 4.2 %collective-permute-done.3 = bf16[2,48,2304]{2,1,0:T(8,128)(2,1)S(1)} collective-permute-done((bf16[2,48,2304]{2,1,0:T(8,128)(2,1)}, bf16[2,48,2304]{2,1,0:T(8,128)(2,1)S(1)}, u32[]{:S(2)}, u32[]{:S(2)}) %collective-permute-start.3) | collective-permute-done | bytes 442400 | tf_op jit(solution)/shard_map/ppermute | solution.py:164
  28.5 0.0 collective-permute-start.7
  28.5 0.6 collective-permute-start.6
  29.1 0.1 collective-permute-start.4
  29.2 4.1 %collective-permute-start.2 = (bf16[48,2304]{1,0:T(8,128)(2,1)S(1)}, bf16[48,2304]{1,0:T(8,128)(2,1)S(1)}, u32[]{:S(2)}, u32[]{:S(2)}) collective-permute-start(bf16[48,2304]{1,0:T(8,128)(2,1)S(1)} %slice_bitcast_fusion.1), channel_id=1, source_target_pairs={{0,1},{1,2},{2,3},{3,0},{4,5},{5,6},{6,7},{7,4},{8,9},{9,10},{10,1... | collective-permute-start | bytes 663560 | tf_op jit(solution)/shard_map/ppermute | solution.py:164
  33.3 0.1 pad_maximum_fusion.1
  33.4 0.0 collective-permute-done.7.rest_1_
  33.4 5.0 %collective-permute-start.9 = (bf16[2,2,48,2304]{3,2,1,0:T(8,128)(2,1)S(1)}, bf16[2,2,48,2304]{3,2,1,0:T(8,128)(2,1)S(1)}, u32[]{:S(2)}, u32[]{:S(2)}) collective-permute-start(bf16[2,2,48,2304]{3,2,1,0:T(8,128)(2,1)S(1)} %pad_maximum_fusion.1), channel_id=1, source_target_pairs={{0,252},{4,8},{8,4},{12,16},{16,12},{20,24},{24,20},{28,32},{32,28... | collective-permute-start | bytes 2654216 | tf_op jit(solution)/shard_map/ppermute | solution.py:174
  38.4 0.0 collective-permute-done.6.rest_0_
  38.4 6.3 %shard_map.245.rest_6_ = f32[2,48,2304]{2,1,0:T(8,128)S(1)} custom-call(bf16[2,48,2304]{2,1,0:T(8,128)(2,1)S(1)} %bitcast.29, bf16[2,48,2304]{2,1,0:T(8,128)(2,1)S(1)} %collective-permute-done.6.rest_0_, bf16[2,48,2304]{2,1,0:T(8,128)(2,1)S(1)} %collective-permute-done.7.rest_1_, f32[2,48,48,128]{3,2,1,0:T(8,128)S(1)} %pad_maximum_fusion.rest_1_.rest_2_, ...), custom_call_target="tpu_custom_call" | custom-call | flops 100000000 | bytes 65536 | tf_op jit(solution)/shard_map/pallas_call | solution.py:127
  44.7 0.0 collective-permute-done.5.rest_0_
  44.8 3.1 %shard_map.246.rest_6_ = f32[2,48,2304]{2,1,0:T(8,128)S(1)} custom-call(bf16[2,48,2304]{2,1,0:T(8,128)(2,1)S(1)} %bitcast.30, bf16[2,48,2304]{2,1,0:T(8,128)(2,1)S(1)} %collective-permute-done.5.rest_0_, f32[2,48,48,128]{3,2,1,0:T(8,128)S(1)} %pad_maximum_fusion.rest_1_.rest_2_, bf16[192,256]{1,0:T(8,128)(2,1)S(1)} %copy-done.1, ...), custom_call_target="tpu_custom_call" | custom-call | flops 100000000 | bytes 65536 | tf_op jit(solution)/shard_map/pallas_call | solution.py:127
  47.9 0.0 collective-permute-done.4
  47.9 0.0 collective-permute-done.2
  48.0 0.1 collective-permute-start.10
  48.1 1.6 %collective-permute-start.8 = (bf16[2,48,2304]{2,1,0:T(8,128)(2,1)S(1)}, bf16[2,48,2304]{2,1,0:T(8,128)(2,1)S(1)}, u32[]{:S(2)}, u32[]{:S(2)}) collective-permute-start(bf16[2,48,2304]{2,1,0:T(8,128)(2,1)S(1)} %pad_maximum_fusion.2), channel_id=1, source_target_pairs={{0,252},{4,8},{8,4},{12,16},{16,12},{20,24},{24,20},{28,32},{32,28... | collective-permute-start | bytes 1327112 | tf_op jit(solution)/shard_map/ppermute | solution.py:174
  49.6 0.2 collective-permute-done.10.rest_0_
  49.8 3.1 %shard_map.247.rest_6_ = f32[2,48,2304]{2,1,0:T(8,128)S(1)} custom-call(bf16[2,48,2304]{2,1,0:T(8,128)(2,1)S(1)} %bitcast.31, bf16[2,48,2304]{2,1,0:T(8,128)(2,1)S(1)} %collective-permute-done.10.rest_0_, f32[2,48,48,128]{3,2,1,0:T(8,128)S(1)} %pad_maximum_fusion.rest_1_.rest_2_, bf16[192,256]{1,0:T(8,128)(2,1)S(1)} %copy-done.1, ...), custom_call_target="tpu_custom_call" | custom-call | flops 100000000 | bytes 65536 | tf_op jit(solution)/shard_map/pallas_call | solution.py:127
  53.0 1.8 %collective-permute-done.9.rest_0_ = bf16[2,2,48,2304]{3,2,1,0:T(8,128)(2,1)S(1)} collective-permute-done((bf16[2,2,48,2304]{3,2,1,0:T(8,128)(2,1)S(1)}, bf16[2,2,48,2304]{3,2,1,0:T(8,128)(2,1)S(1)}, u32[]{:S(2)}, u32[]{:S(2)}) %collective-permute-start.9) | collective-permute-done | bytes 884768 | tf_op jit(solution)/shard_map/ppermute | solution.py:174
  54.7 6.3 %shard_map.248.rest_6_ = f32[2,48,2304]{2,1,0:T(8,128)S(1)} custom-call(bf16[2,48,2304]{2,1,0:T(8,128)(2,1)S(1)} %bitcast.32, bf16[2,2,48,2304]{3,2,1,0:T(8,128)(2,1)S(1)} %collective-permute-done.9.rest_0_, f32[2,48,48,128]{3,2,1,0:T(8,128)S(1)} %pad_maximum_fusion.rest_1_.rest_2_, bf16[192,256]{1,0:T(8,128)(2,1)S(1)} %copy-done.1, ...), custom_call_target="tpu_custom_call" | custom-call | flops 100000000 | bytes 65536 | tf_op jit(solution)/shard_map/pallas_call | solution.py:127
  61.1 0.0 collective-permute-done.8.rest_0_
  61.1 4.0 %shard_map.249 = f32[2,48,2304]{2,1,0:T(8,128)} custom-call(bf16[2,48,2304]{2,1,0:T(8,128)(2,1)S(1)} %bitcast.33, bf16[2,48,2304]{2,1,0:T(8,128)(2,1)S(1)} %collective-permute-done.8.rest_0_, f32[2,48,48,128]{3,2,1,0:T(8,128)S(1)} %pad_maximum_fusion.rest_1_.rest_2_, bf16[192,256]{1,0:T(8,128)(2,1)S(1)} %copy-done.1, bf16[96,144]{1,0:T(8,128)(2,1)S(1)} %copy-done.3, ...), custom_call_target="tpu_custom_call" | custom-call | flops 100000000 | bytes 65536 | tf_op jit(solution)/shard_map/pallas_call | solution.py:127
  (6 shorter events, 0.1 us)
Async XLA Ops:
  0.0 16.9 %collective-permute-start.1 = (bf16[2,48,2304]{2,1,0:T(8,128)(2,1)}, bf16[2,48,2304]{2,1,0:T(8,128)(2,1)S(1)}, u32[]{:S(2)}, u32[]{:S(2)}) collective-permute-start(bf16[2,48,2304]{2,1,0:T(8,128)(2,1)} %bitcast.24), channel_id=1, source_target_pairs={{0,4},{4,0},{8,12},{12,8},{16,20},{20,16},{24,28},{28,24},{32,36},... | collective-permute-start | bytes 1327112 | tf_op jit(solution)/shard_map/ppermute | solution.py:169
  0.0 24.3 %collective-permute-start = (bf16[2,48,2304]{2,1,0:T(8,128)(2,1)}, bf16[2,48,2304]{2,1,0:T(8,128)(2,1)S(1)}, u32[]{:S(2)}, u32[]{:S(2)}) collective-permute-start(bf16[2,48,2304]{2,1,0:T(8,128)(2,1)} %bitcast.25), channel_id=1, source_target_pairs={{0,1},{1,2},{2,3},{3,0},{4,5},{5,6},{6,7},{7,4},{8,9},{9,10},{10,1... | collective-permute-start | bytes 1327112 | tf_op jit(solution)/shard_map/ppermute | solution.py:164
  4.5 24.0 %collective-permute-start.3 = (bf16[2,48,2304]{2,1,0:T(8,128)(2,1)}, bf16[2,48,2304]{2,1,0:T(8,128)(2,1)S(1)}, u32[]{:S(2)}, u32[]{:S(2)}) collective-permute-start(bf16[2,48,2304]{2,1,0:T(8,128)(2,1)} %bitcast.26), channel_id=1, source_target_pairs={{0,3},{1,0},{2,1},{3,2},{4,7},{5,4},{6,5},{7,6},{8,11},{9,8},{10,9... | collective-permute-start | bytes 1327112 | tf_op jit(solution)/shard_map/ppermute | solution.py:164
  4.5 40.3 %collective-permute-start.5 = (bf16[2,48,2304]{2,1,0:T(8,128)(2,1)}, bf16[2,48,2304]{2,1,0:T(8,128)(2,1)S(1)}, u32[]{:S(2)}, u32[]{:S(2)}) collective-permute-start(bf16[2,48,2304]{2,1,0:T(8,128)(2,1)} %bitcast.27), channel_id=1, source_target_pairs={{0,252},{4,8},{8,4},{12,16},{16,12},{20,24},{24,20},{28,32},{32,28... | collective-permute-start | bytes 1327112 | tf_op jit(solution)/shard_map/ppermute | solution.py:174
  16.6 1.0 %copy-start = (bf16[1,2,1,48,2304]{4,3,2,1,0:T(8,128)(2,1)S(1)}, bf16[1,2,1,48,2304]{4,3,2,1,0:T(8,128)(2,1)}, u32[]{:S(2)}) copy-start(bf16[1,2,1,48,2304]{4,3,2,1,0:T(8,128)(2,1)} %param.26) | copy-start | bytes 1327108
  16.7 1.0 %copy-start.1 = (bf16[192,256]{1,0:T(8,128)(2,1)S(1)}, bf16[192,256]{1,0:T(8,128)(2,1)}, u32[]{:S(2)}) copy-start(bf16[192,256]{1,0:T(8,128)(2,1)} %constant.131.clone.rest_2_.rest_3_) | copy-start | bytes 294916
  16.7 1.1 %copy-start.2 = (bf16[192,256]{1,0:T(8,128)(2,1)S(1)}, bf16[192,256]{1,0:T(8,128)(2,1)}, u32[]{:S(2)}) copy-start(bf16[192,256]{1,0:T(8,128)(2,1)} %constant.134.clone.rest_5_.rest_6_) | copy-start | bytes 294916
  16.7 1.0 %copy-start.3 = (bf16[96,144]{1,0:T(8,128)(2,1)S(1)}, bf16[96,144]{1,0:T(8,128)(2,1)}, u32[]{:S(2)}) copy-start(bf16[96,144]{1,0:T(8,128)(2,1)} %constant.132.clone.rest_3_.rest_4_) | copy-start | bytes 82948
  16.7 1.0 %copy-start.4 = (bf16[96,144]{1,0:T(8,128)(2,1)S(1)}, bf16[96,144]{1,0:T(8,128)(2,1)}, u32[]{:S(2)}) copy-start(bf16[96,144]{1,0:T(8,128)(2,1)} %constant.133.clone.rest_4_.rest_5_) | copy-start | bytes 82948
  28.5 4.9 %collective-permute-start.7 = (bf16[2,48,2304]{2,1,0:T(8,128)(2,1)S(1)}, bf16[2,48,2304]{2,1,0:T(8,128)(2,1)S(1)}, u32[]{:S(2)}, u32[]{:S(2)}) collective-permute-start(bf16[2,48,2304]{2,1,0:T(8,128)(2,1)S(1)} %collective-permute-done.3), channel_id=1, source_target_pairs={{0,4},{4,0},{8,12},{12,8},{16,20},{20,16},{24,28},{28,24},{32,36},... | collective-permute-start | bytes 1327112 | tf_op jit(solution)/shard_map/ppermute | solution.py:169
  28.5 9.9 %collective-permute-start.6 = (bf16[2,48,2304]{2,1,0:T(8,128)(2,1)S(1)}, bf16[2,48,2304]{2,1,0:T(8,128)(2,1)S(1)}, u32[]{:S(2)}, u32[]{:S(2)}) collective-permute-start(bf16[2,48,2304]{2,1,0:T(8,128)(2,1)S(1)} %collective-permute-done), channel_id=1, source_target_pairs={{0,4},{4,0},{8,12},{12,8},{16,20},{20,16},{24,28},{28,24},{32,36},... | collective-permute-start | bytes 1327112 | tf_op jit(solution)/shard_map/ppermute | solution.py:169
  29.1 18.8 %collective-permute-start.4 = (bf16[48,2304]{1,0:T(8,128)(2,1)S(1)}, bf16[48,2304]{1,0:T(8,128)(2,1)S(1)}, u32[]{:S(2)}, u32[]{:S(2)}) collective-permute-start(bf16[48,2304]{1,0:T(8,128)(2,1)S(1)} %slice_bitcast_fusion), channel_id=1, source_target_pairs={{0,3},{1,0},{2,1},{3,2},{4,7},{5,4},{6,5},{7,6},{8,11},{9,8},{10,9... | collective-permute-start | bytes 663560 | tf_op jit(solution)/shard_map/ppermute | solution.py:164
  29.2 18.7 %collective-permute-start.2 = (bf16[48,2304]{1,0:T(8,128)(2,1)S(1)}, bf16[48,2304]{1,0:T(8,128)(2,1)S(1)}, u32[]{:S(2)}, u32[]{:S(2)}) collective-permute-start(bf16[48,2304]{1,0:T(8,128)(2,1)S(1)} %slice_bitcast_fusion.1), channel_id=1, source_target_pairs={{0,1},{1,2},{2,3},{3,0},{4,5},{5,6},{6,7},{7,4},{8,9},{9,10},{10,1... | collective-permute-start | bytes 663560 | tf_op jit(solution)/shard_map/ppermute | solution.py:164
  33.4 21.3 %collective-permute-start.9 = (bf16[2,2,48,2304]{3,2,1,0:T(8,128)(2,1)S(1)}, bf16[2,2,48,2304]{3,2,1,0:T(8,128)(2,1)S(1)}, u32[]{:S(2)}, u32[]{:S(2)}) collective-permute-start(bf16[2,2,48,2304]{3,2,1,0:T(8,128)(2,1)S(1)} %pad_maximum_fusion.1), channel_id=1, source_target_pairs={{0,252},{4,8},{8,4},{12,16},{16,12},{20,24},{24,20},{28,32},{32,28... | collective-permute-start | bytes 2654216 | tf_op jit(solution)/shard_map/ppermute | solution.py:174
  48.0 1.9 %collective-permute-start.10 = (bf16[2,48,2304]{2,1,0:T(8,128)(2,1)S(1)}, bf16[2,48,2304]{2,1,0:T(8,128)(2,1)S(1)}, u32[]{:S(2)}, u32[]{:S(2)}) collective-permute-start(bf16[2,48,2304]{2,1,0:T(8,128)(2,1)S(1)} %pad_maximum_fusion.2), channel_id=1, source_target_pairs={{0,4},{4,0},{8,12},{12,8},{16,20},{20,16},{24,28},{28,24},{32,36},... | collective-permute-start | bytes 1327112 | tf_op jit(solution)/shard_map/ppermute | solution.py:169
  48.1 13.0 %collective-permute-start.8 = (bf16[2,48,2304]{2,1,0:T(8,128)(2,1)S(1)}, bf16[2,48,2304]{2,1,0:T(8,128)(2,1)S(1)}, u32[]{:S(2)}, u32[]{:S(2)}) collective-permute-start(bf16[2,48,2304]{2,1,0:T(8,128)(2,1)S(1)} %pad_maximum_fusion.2), channel_id=1, source_target_pairs={{0,252},{4,8},{8,4},{12,16},{16,12},{20,24},{24,20},{28,32},{32,28... | collective-permute-start | bytes 1327112 | tf_op jit(solution)/shard_map/ppermute | solution.py:174

commit v5 on v3

--- a/solution.py
+++ b/solution.py
@@ -65,7 +65,9 @@
     def _():
         acc_ref[...] = jnp.zeros_like(acc_ref) if first else acc_in_ref[...]
 
-    for at, field in enumerate(fields):
+    if len(fields) == 1:
+        cur = fields[0]
+    for at, field in enumerate(fields if len(fields) > 1 else []):
 
         @pl.when(f == at)
         def _():

time: 65.3 us -> 65.3 us (level)
  no operation moved by 1% of the time
where the time goes in v5:
time: 65.3 us; the launch traced here: 65.2 us
  Pallas kernels  26 us (40%)
  starting transfers between devices  20.8 us (32%)
  waiting for transfers between devices  10.3 us (16%)
  other arithmetic  5.75 us (9%)
  local copies, waits for them, and re-layouts  2.09 us (3%)
    pallas_call x6, Pallas kernels, convolve(): pl.pallas_call(functools.partial(kernel, first, tuple(places)), grid=(len...  26 us
    ppermute x3, starting transfers between devices, swap_next(): lax.ppermute(value, 'kpool', [(i, (i + 1 if i % 2 else i - 1) % n) for i...  11.9 us
    ppermute x4, starting transfers between devices, band_hop(): return lax.ppermute(value, 'band', [(i, (i + by) % n) for i in range(n)])  8.69 us
    ppermute x4, waiting for transfers between devices, band_hop(): return lax.ppermute(value, 'band', [(i, (i + by) % n) for i in range(n)])  7.62 us
    ppermute x3, waiting for transfers between devices, swap_next(): lax.ppermute(value, 'kpool', [(i, (i + 1 if i % 2 else i - 1) % n) for i...  2.17 us
    integer_pow x2, other arithmetic, coulomb_zyx(): ay = (offset[1] + freq) ** 2  1.32 us
  transfers between devices with their start and end apart: 10, of which 4 were waited for; matrix products, arithmetic and copies ran while one was open for 11% of the time, Pallas kernels for 34%

profile of v5, /device:TPU:64, one launch (start us, length us, event | category | flops | bytes accessed | tf_op | source)
XLA Modules:
  0.0 65.2 jit_solution(3540056394494144038)
XLA Ops:
  0.0 0.0 collective-permute-start.1
  0.0 4.5 %collective-permute-start = (bf16[2,48,2304]{2,1,0:T(8,128)(2,1)}, bf16[2,48,2304]{2,1,0:T(8,128)(2,1)S(1)}, u32[]{:S(2)}, u32[]{:S(2)}) collective-permute-start(bf16[2,48,2304]{2,1,0:T(8,128)(2,1)} %bitcast.25), channel_id=1, source_target_pairs={{0,1},{1,2},{2,3},{3,0},{4,5},{5,6},{6,7},{7,4},{8,9},{9,10},{10,1... | collective-permute-start | bytes 1327112 | tf_op jit(solution)/shard_map/ppermute | solution.py:166
  4.5 0.0 collective-permute-start.3
  4.5 5.5 %collective-permute-start.5 = (bf16[2,48,2304]{2,1,0:T(8,128)(2,1)}, bf16[2,48,2304]{2,1,0:T(8,128)(2,1)S(1)}, u32[]{:S(2)}, u32[]{:S(2)}) collective-permute-start(bf16[2,48,2304]{2,1,0:T(8,128)(2,1)} %bitcast.27), channel_id=1, source_target_pairs={{0,252},{4,8},{8,4},{12,16},{16,12},{20,24},{24,20},{28,32},{32,28... | collective-permute-start | bytes 1327112 | tf_op jit(solution)/shard_map/ppermute | solution.py:176
  10.0 0.7 %fusion.5 = (s32[64,1]{0,1:T(1,128)S(1)}, s32[64,1]{0,1:T(1,128)S(1)}, s32[64,1]{0,1:T(1,128)S(1)}) fusion(s32[64]{0:T(128)} %param.27), kind=kLoop, calls=%fused_computation.35 | loop fusion | flops 2560 | bytes 1024 | tf_op jit(solution)/shard_map/stack | solution.py:161
  10.7 0.1 dynamic-slice_subtract_fusion.1
  10.8 0.6 fusion.11
  11.4 0.6 fusion.12
  12.0 0.7 %add_multiply_fusion.1 = f32[48]{0:T(128)S(1)} fusion(f32[]{:T(128)} %bitcast.8), kind=kLoop, calls=%fused_computation.41 | loop fusion | flops 288 | bytes 196 | tf_op jit(solution)/shard_map/integer_pow | solution.py:149
  12.7 0.6 add_multiply_fusion.4
  13.3 1.3 %add_multiply_fusion.2 = (f32[128]{0:T(128)S(1)}, f32[128]{0:T(128)S(1)}) fusion(f32[]{:T(128)} %bitcast.7, f32[]{:T(128)} %bitcast.4), kind=kLoop, calls=%fused_computation.42 | loop fusion | flops 1792 | bytes 1032 | tf_op jit(solution)/shard_map/integer_pow | solution.py:148
  14.6 0.1 broadcast_add_fusion
  14.7 0.1 broadcast_add_fusion.1
  14.7 1.3 %add_multiply_fusion = (f32[48]{0:T(128)S(1)}, f32[48]{0:T(128)S(1)}) fusion(f32[]{:T(128)} %bitcast.9, f32[]{:T(128)} %bitcast.6), kind=kLoop, calls=%fused_computation.40 | loop fusion | flops 384 | bytes 392 | tf_op jit(solution)/shard_map/integer_pow | solution.py:150
  16.0 0.1 broadcast_or_fusion
  16.1 0.6 fusion.1
  16.7 0.0 copy-start
  16.7 0.0 copy-start.1
  16.7 0.0 copy-start.2
  16.7 0.0 copy-start.3
  16.8 0.0 copy-start.4
  16.8 0.2 pad_maximum_fusion.rest_1_
  16.9 0.0 collective-permute-done.1.rest_0_
  16.9 0.8 %copy-done = bf16[1,2,1,48,2304]{4,3,2,1,0:T(8,128)(2,1)S(1)} copy-done((bf16[1,2,1,48,2304]{4,3,2,1,0:T(8,128)(2,1)S(1)}, bf16[1,2,1,48,2304]{4,3,2,1,0:T(8,128)(2,1)}, u32[]{:S(2)}) %copy-start) | copy-done | bytes 442392
  17.7 0.0 copy-done.1
  17.7 0.0 copy-done.2
  17.8 0.0 copy-done.3
  17.8 0.0 copy-done.4
  17.8 3.1 %shard_map.244.rest_6_ = f32[2,48,2304]{2,1,0:T(8,128)S(1)} custom-call(bf16[2,48,2304]{2,1,0:T(8,128)(2,1)S(1)} %bitcast.28, bf16[2,48,2304]{2,1,0:T(8,128)(2,1)S(1)} %collective-permute-done.1.rest_0_, f32[2,48,48,128]{3,2,1,0:T(8,128)S(1)} %pad_maximum_fusion.rest_1_, bf16[192,256]{1,0:T(8,128)(2,1)S(1)} %copy-done.1, bf16[96,144]{1,0:T(8,128)(2,1)S(1)} %copy-done.3, ...), custom_call_target="tpu_custom_call" | custom-call | flops 100000000 | bytes 65536 | tf_op jit(solution)/shard_map/pallas_call | solution.py:129
  20.9 3.4 %collective-permute-done = bf16[2,48,2304]{2,1,0:T(8,128)(2,1)S(1)} collective-permute-done((bf16[2,48,2304]{2,1,0:T(8,128)(2,1)}, bf16[2,48,2304]{2,1,0:T(8,128)(2,1)S(1)}, u32[]{:S(2)}, u32[]{:S(2)}) %collective-permute-start) | collective-permute-done | bytes 442400 | tf_op jit(solution)/shard_map/ppermute | solution.py:166
  24.3 4.2 %collective-permute-done.3 = bf16[2,48,2304]{2,1,0:T(8,128)(2,1)S(1)} collective-permute-done((bf16[2,48,2304]{2,1,0:T(8,128)(2,1)}, bf16[2,48,2304]{2,1,0:T(8,128)(2,1)S(1)}, u32[]{:S(2)}, u32[]{:S(2)}) %collective-permute-start.3) | collective-permute-done | bytes 442400 | tf_op jit(solution)/shard_map/ppermute | solution.py:166
  28.5 0.1 pad_maximum_fusion.1
  28.6 0.1 collective-permute-start.6
  28.7 0.1 collective-permute-start.4
  28.8 4.1 %collective-permute-start.2 = (bf16[48,2304]{1,0:T(8,128)(2,1)S(1)}, bf16[48,2304]{1,0:T(8,128)(2,1)S(1)}, u32[]{:S(2)}, u32[]{:S(2)}) collective-permute-start(bf16[48,2304]{1,0:T(8,128)(2,1)S(1)} %slice_bitcast_fusion.1), channel_id=1, source_target_pairs={{0,1},{1,2},{2,3},{3,0},{4,5},{5,6},{6,7},{7,4},{8,9},{9,10},{10,1... | collective-permute-start | bytes 663560 | tf_op jit(solution)/shard_map/ppermute | solution.py:166
  32.9 5.2 %collective-permute-start.8 = (bf16[2,2,48,2304]{3,2,1,0:T(8,128)(2,1)S(1)}, bf16[2,2,48,2304]{3,2,1,0:T(8,128)(2,1)S(1)}, u32[]{:S(2)}, u32[]{:S(2)}) collective-permute-start(bf16[2,2,48,2304]{3,2,1,0:T(8,128)(2,1)S(1)} %pad_maximum_fusion.1), channel_id=1, source_target_pairs={{0,252},{4,8},{8,4},{12,16},{16,12},{20,24},{24,20},{28,32},{32,28... | collective-permute-start | bytes 2654216 | tf_op jit(solution)/shard_map/ppermute | solution.py:176
  38.1 0.0 collective-permute-done.6.rest_0_
  38.1 6.3 %shard_map.245.rest_6_ = f32[2,48,2304]{2,1,0:T(8,128)S(1)} custom-call(bf16[2,48,2304]{2,1,0:T(8,128)(2,1)S(1)} %bitcast.29, bf16[2,2,48,2304]{3,2,1,0:T(8,128)(2,1)S(1)} %collective-permute-done.6.rest_0_, f32[2,48,48,128]{3,2,1,0:T(8,128)S(1)} %pad_maximum_fusion.rest_1_, bf16[192,256]{1,0:T(8,128)(2,1)S(1)} %copy-done.1, bf16[96,144]{1,0:T(8,128)(2,1)S(1)} %copy-done.3, ...), custom_call_target="tpu_custom_call" | custom-call | flops 100000000 | bytes 65536 | tf_op jit(solution)/shard_map/pallas_call | solution.py:129
  44.5 0.0 collective-permute-done.5.rest_0_
  44.5 3.1 %shard_map.246.rest_6_ = f32[2,48,2304]{2,1,0:T(8,128)S(1)} custom-call(bf16[2,48,2304]{2,1,0:T(8,128)(2,1)S(1)} %bitcast.30, bf16[2,48,2304]{2,1,0:T(8,128)(2,1)S(1)} %collective-permute-done.5.rest_0_, f32[2,48,48,128]{3,2,1,0:T(8,128)S(1)} %pad_maximum_fusion.rest_1_, bf16[192,256]{1,0:T(8,128)(2,1)S(1)} %copy-done.1, bf16[96,144]{1,0:T(8,128)(2,1)S(1)} %copy-done.3, ...), custom_call_target="tpu_custom_call" | custom-call | flops 100000000 | bytes 65536 | tf_op jit(solution)/shard_map/pallas_call | solution.py:129
  47.6 0.0 collective-permute-done.4
  47.6 0.0 collective-permute-done.2
  47.7 0.1 collective-permute-start.9
  47.8 1.2 %collective-permute-start.7 = (bf16[2,48,2304]{2,1,0:T(8,128)(2,1)S(1)}, bf16[2,48,2304]{2,1,0:T(8,128)(2,1)S(1)}, u32[]{:S(2)}, u32[]{:S(2)}) collective-permute-start(bf16[2,48,2304]{2,1,0:T(8,128)(2,1)S(1)} %pad_maximum_fusion.2), channel_id=1, source_target_pairs={{0,252},{4,8},{8,4},{12,16},{16,12},{20,24},{24,20},{28,32},{32,28... | collective-permute-start | bytes 1327112 | tf_op jit(solution)/shard_map/ppermute | solution.py:176
  49.0 0.5 collective-permute-done.9.rest_0_
  49.5 3.1 %shard_map.247.rest_6_ = f32[2,48,2304]{2,1,0:T(8,128)S(1)} custom-call(bf16[2,48,2304]{2,1,0:T(8,128)(2,1)S(1)} %bitcast.31, bf16[2,48,2304]{2,1,0:T(8,128)(2,1)S(1)} %collective-permute-done.9.rest_0_, f32[2,48,48,128]{3,2,1,0:T(8,128)S(1)} %pad_maximum_fusion.rest_1_, bf16[192,256]{1,0:T(8,128)(2,1)S(1)} %copy-done.1, bf16[96,144]{1,0:T(8,128)(2,1)S(1)} %copy-done.3, ...), custom_call_target="tpu_custom_call" | custom-call | flops 100000000 | bytes 65536 | tf_op jit(solution)/shard_map/pallas_call | solution.py:129
  52.6 2.2 %collective-permute-done.8.rest_0_ = bf16[2,2,48,2304]{3,2,1,0:T(8,128)(2,1)S(1)} collective-permute-done((bf16[2,2,48,2304]{3,2,1,0:T(8,128)(2,1)S(1)}, bf16[2,2,48,2304]{3,2,1,0:T(8,128)(2,1)S(1)}, u32[]{:S(2)}, u32[]{:S(2)}) %collective-permute-start.8) | collective-permute-done | bytes 884768 | tf_op jit(solution)/shard_map/ppermute | solution.py:176
  54.8 6.3 %shard_map.248.rest_6_ = f32[2,48,2304]{2,1,0:T(8,128)S(1)} custom-call(bf16[2,48,2304]{2,1,0:T(8,128)(2,1)S(1)} %bitcast.32, bf16[2,2,48,2304]{3,2,1,0:T(8,128)(2,1)S(1)} %collective-permute-done.8.rest_0_, f32[2,48,48,128]{3,2,1,0:T(8,128)S(1)} %pad_maximum_fusion.rest_1_, bf16[192,256]{1,0:T(8,128)(2,1)S(1)} %copy-done.1, bf16[96,144]{1,0:T(8,128)(2,1)S(1)} %copy-done.3, ...), custom_call_target="tpu_custom_call" | custom-call | flops 100000000 | bytes 65536 | tf_op jit(solution)/shard_map/pallas_call | solution.py:129
  61.1 0.0 collective-permute-done.7.rest_0_
  61.1 4.0 %shard_map.249 = f32[2,48,2304]{2,1,0:T(8,128)} custom-call(bf16[2,48,2304]{2,1,0:T(8,128)(2,1)S(1)} %bitcast.33, bf16[2,48,2304]{2,1,0:T(8,128)(2,1)S(1)} %collective-permute-done.7.rest_0_, f32[2,48,48,128]{3,2,1,0:T(8,128)S(1)} %pad_maximum_fusion.rest_1_, bf16[192,256]{1,0:T(8,128)(2,1)S(1)} %copy-done.1, bf16[96,144]{1,0:T(8,128)(2,1)S(1)} %copy-done.3, ...), custom_call_target="tpu_custom_call" | custom-call | flops 100000000 | bytes 65536 | tf_op jit(solution)/shard_map/pallas_call | solution.py:129
  (6 shorter events, 0.1 us)
Async XLA Ops:
  0.0 16.9 %collective-permute-start.1 = (bf16[2,48,2304]{2,1,0:T(8,128)(2,1)}, bf16[2,48,2304]{2,1,0:T(8,128)(2,1)S(1)}, u32[]{:S(2)}, u32[]{:S(2)}) collective-permute-start(bf16[2,48,2304]{2,1,0:T(8,128)(2,1)} %bitcast.24), channel_id=1, source_target_pairs={{0,4},{4,0},{8,12},{12,8},{16,20},{20,16},{24,28},{28,24},{32,36},... | collective-permute-start | bytes 1327112 | tf_op jit(solution)/shard_map/ppermute | solution.py:171
  0.0 24.3 %collective-permute-start = (bf16[2,48,2304]{2,1,0:T(8,128)(2,1)}, bf16[2,48,2304]{2,1,0:T(8,128)(2,1)S(1)}, u32[]{:S(2)}, u32[]{:S(2)}) collective-permute-start(bf16[2,48,2304]{2,1,0:T(8,128)(2,1)} %bitcast.25), channel_id=1, source_target_pairs={{0,1},{1,2},{2,3},{3,0},{4,5},{5,6},{6,7},{7,4},{8,9},{9,10},{10,1... | collective-permute-start | bytes 1327112 | tf_op jit(solution)/shard_map/ppermute | solution.py:166
  4.5 24.0 %collective-permute-start.3 = (bf16[2,48,2304]{2,1,0:T(8,128)(2,1)}, bf16[2,48,2304]{2,1,0:T(8,128)(2,1)S(1)}, u32[]{:S(2)}, u32[]{:S(2)}) collective-permute-start(bf16[2,48,2304]{2,1,0:T(8,128)(2,1)} %bitcast.26), channel_id=1, source_target_pairs={{0,3},{1,0},{2,1},{3,2},{4,7},{5,4},{6,5},{7,6},{8,11},{9,8},{10,9... | collective-permute-start | bytes 1327112 | tf_op jit(solution)/shard_map/ppermute | solution.py:166
  4.5 40.0 %collective-permute-start.5 = (bf16[2,48,2304]{2,1,0:T(8,128)(2,1)}, bf16[2,48,2304]{2,1,0:T(8,128)(2,1)S(1)}, u32[]{:S(2)}, u32[]{:S(2)}) collective-permute-start(bf16[2,48,2304]{2,1,0:T(8,128)(2,1)} %bitcast.27), channel_id=1, source_target_pairs={{0,252},{4,8},{8,4},{12,16},{16,12},{20,24},{24,20},{28,32},{32,28... | collective-permute-start | bytes 1327112 | tf_op jit(solution)/shard_map/ppermute | solution.py:176
  16.7 1.0 %copy-start = (bf16[1,2,1,48,2304]{4,3,2,1,0:T(8,128)(2,1)S(1)}, bf16[1,2,1,48,2304]{4,3,2,1,0:T(8,128)(2,1)}, u32[]{:S(2)}) copy-start(bf16[1,2,1,48,2304]{4,3,2,1,0:T(8,128)(2,1)} %param.26) | copy-start | bytes 1327108
  16.7 1.0 %copy-start.1 = (bf16[192,256]{1,0:T(8,128)(2,1)S(1)}, bf16[192,256]{1,0:T(8,128)(2,1)}, u32[]{:S(2)}) copy-start(bf16[192,256]{1,0:T(8,128)(2,1)} %constant.131.clone.rest_2_) | copy-start | bytes 294916
  16.7 1.1 %copy-start.2 = (bf16[192,256]{1,0:T(8,128)(2,1)S(1)}, bf16[192,256]{1,0:T(8,128)(2,1)}, u32[]{:S(2)}) copy-start(bf16[192,256]{1,0:T(8,128)(2,1)} %constant.134.clone.rest_5_) | copy-start | bytes 294916
  16.7 1.0 %copy-start.3 = (bf16[96,144]{1,0:T(8,128)(2,1)S(1)}, bf16[96,144]{1,0:T(8,128)(2,1)}, u32[]{:S(2)}) copy-start(bf16[96,144]{1,0:T(8,128)(2,1)} %constant.132.clone.rest_3_) | copy-start | bytes 82948
  16.8 1.0 %copy-start.4 = (bf16[96,144]{1,0:T(8,128)(2,1)S(1)}, bf16[96,144]{1,0:T(8,128)(2,1)}, u32[]{:S(2)}) copy-start(bf16[96,144]{1,0:T(8,128)(2,1)} %constant.133.clone.rest_4_) | copy-start | bytes 82948
  28.6 9.5 %collective-permute-start.6 = (bf16[2,2,48,2304]{3,2,1,0:T(8,128)(2,1)S(1)}, bf16[2,2,48,2304]{3,2,1,0:T(8,128)(2,1)S(1)}, u32[]{:S(2)}, u32[]{:S(2)}) collective-permute-start(bf16[2,2,48,2304]{3,2,1,0:T(8,128)(2,1)S(1)} %pad_maximum_fusion.1), channel_id=1, source_target_pairs={{0,4},{4,0},{8,12},{12,8},{16,20},{20,16},{24,28},{28,24},{32,36},... | collective-permute-start | bytes 2654216 | tf_op jit(solution)/shard_map/ppermute | solution.py:171
  28.7 18.8 %collective-permute-start.4 = (bf16[48,2304]{1,0:T(8,128)(2,1)S(1)}, bf16[48,2304]{1,0:T(8,128)(2,1)S(1)}, u32[]{:S(2)}, u32[]{:S(2)}) collective-permute-start(bf16[48,2304]{1,0:T(8,128)(2,1)S(1)} %slice_bitcast_fusion), channel_id=1, source_target_pairs={{0,3},{1,0},{2,1},{3,2},{4,7},{5,4},{6,5},{7,6},{8,11},{9,8},{10,9... | collective-permute-start | bytes 663560 | tf_op jit(solution)/shard_map/ppermute | solution.py:166
  28.8 18.8 %collective-permute-start.2 = (bf16[48,2304]{1,0:T(8,128)(2,1)S(1)}, bf16[48,2304]{1,0:T(8,128)(2,1)S(1)}, u32[]{:S(2)}, u32[]{:S(2)}) collective-permute-start(bf16[48,2304]{1,0:T(8,128)(2,1)S(1)} %slice_bitcast_fusion.1), channel_id=1, source_target_pairs={{0,1},{1,2},{2,3},{3,0},{4,5},{5,6},{6,7},{7,4},{8,9},{9,10},{10,1... | collective-permute-start | bytes 663560 | tf_op jit(solution)/shard_map/ppermute | solution.py:166
  32.9 21.9 %collective-permute-start.8 = (bf16[2,2,48,2304]{3,2,1,0:T(8,128)(2,1)S(1)}, bf16[2,2,48,2304]{3,2,1,0:T(8,128)(2,1)S(1)}, u32[]{:S(2)}, u32[]{:S(2)}) collective-permute-start(bf16[2,2,48,2304]{3,2,1,0:T(8,128)(2,1)S(1)} %pad_maximum_fusion.1), channel_id=1, source_target_pairs={{0,252},{4,8},{8,4},{12,16},{16,12},{20,24},{24,20},{28,32},{32,28... | collective-permute-start | bytes 2654216 | tf_op jit(solution)/shard_map/ppermute | solution.py:176
  47.7 1.9 %collective-permute-start.9 = (bf16[2,48,2304]{2,1,0:T(8,128)(2,1)S(1)}, bf16[2,48,2304]{2,1,0:T(8,128)(2,1)S(1)}, u32[]{:S(2)}, u32[]{:S(2)}) collective-permute-start(bf16[2,48,2304]{2,1,0:T(8,128)(2,1)S(1)} %pad_maximum_fusion.2), channel_id=1, source_target_pairs={{0,4},{4,0},{8,12},{12,8},{16,20},{20,16},{24,28},{28,24},{32,36},... | collective-permute-start | bytes 1327112 | tf_op jit(solution)/shard_map/ppermute | solution.py:171
  47.8 13.4 %collective-permute-start.7 = (bf16[2,48,2304]{2,1,0:T(8,128)(2,1)S(1)}, bf16[2,48,2304]{2,1,0:T(8,128)(2,1)S(1)}, u32[]{:S(2)}, u32[]{:S(2)}) collective-permute-start(bf16[2,48,2304]{2,1,0:T(8,128)(2,1)S(1)} %pad_maximum_fusion.2), channel_id=1, source_target_pairs={{0,252},{4,8},{8,4},{12,16},{16,12},{20,24},{24,20},{28,32},{32,28... | collective-permute-start | bytes 1327112 | tf_op jit(solution)/shard_map/ppermute | solution.py:176
